TPU v7x, 128 devices: a whole 4x4x4 slice. The times are simulated.
128 devices in a mesh: expert: 4 (over y), shard: 32 (over z, x, core).
Axes of the slice: x: 4, y: 4, z: 4, core: 2. Of those that a mesh axis runs over, the one named last changes fastest.
Arguments:
- gradient: float32 [4, 32, 512, 512], P('expert', None, 'shard')
- left_stat: float32 [4, 96, 512, 512], P('expert', 'shard'), as said below
- right_stat: float32 [4, 96, 512, 512], P('expert', 'shard'), as said below
- assign: int32 [4, 96], P('expert'), may hold values from -1 to 31, as said below
Outputs:
- update: float32 [4, 32, 512, 512], P('expert', None, 'shard')
- new_left: float32 [4, 96, 512, 512], P('expert', 'shard')
- new_right: float32 [4, 96, 512, 512], P('expert', 'shard')
Inputs may be any that keep to these rules, and one draw needn't show every extreme that they name: `assign`: slots d * 3 to d * 3 + 2 are those of device d of shard; each holds a block id or -1, the ids first and the -1 after. Every block of an expert is in exactly one slot. In every expert some device holds 3 blocks. `left_stat`: symmetric positive definite. `right_stat`: symmetric positive definite.
All inputs are finite; a program needn't handle non-finite values.
Results may differ from a plain program's by a relative error of at most 0.00018.
Values sent between devices are 32-bit elements; how exact they have to be, the bound alone decides.
A program may use at most 128 MiB of HBM per device.

v0:
```python
import jax
import jax.numpy as jnp
from jax import lax
from jax.sharding import PartitionSpec as P

beta_decay = 0.95
clip_rms = 1.0


def product(left_mat, right_mat):
    return jnp.dot(
        left_mat, right_mat, precision=lax.Precision.HIGHEST, preferred_element_type=jnp.float32
    )


def inverse_root(matrix):
    identity = jnp.eye(matrix.shape[0], dtype=jnp.float32)
    norm_fourth = jnp.sqrt(jnp.sum(matrix * matrix) + 1e-06)
    root_scale = jnp.sqrt(jnp.sqrt(norm_fourth))
    scaled_start = matrix / norm_fourth
    first_step = (5.0 * identity - scaled_start) * 0.25
    square = product(first_step, first_step)
    fourth = product(square, square)
    moved_mat = product(fourth, scaled_start)
    second_step = (5.0 * identity - moved_mat) * 0.25
    return product(first_step / root_scale, second_step)


def precondition(scaled, left_new, right_new):
    precond = product(product(inverse_root(left_new), scaled), inverse_root(right_new))
    graft_ratio = jnp.sqrt(jnp.mean(scaled * scaled) + 1e-12) / jnp.sqrt(
        jnp.mean(precond * precond) + 1e-12
    )
    return precond * graft_ratio


def body(gradient, left_stat, right_stat, assign):
    local_grad = gradient[0]
    left_held = left_stat[0]
    right_held = right_stat[0]
    assign_row = assign[0]
    shards = lax.axis_size("shard")
    my_index = lax.axis_index("shard")
    block_count, row_count, width = local_grad.shape
    owned_slots = left_held.shape[0]
    slot_grid = assign_row.reshape(shards, owned_slots)
    partial_sum = jnp.sum(local_grad * local_grad)
    total_sum = lax.psum(partial_sum, ("expert", "shard"))
    entries = float(local_grad.size * shards * lax.axis_size("expert"))
    factor = jnp.minimum(1.0, clip_rms / jnp.sqrt(total_sum / entries + 1e-06))
    live_slots = slot_grid >= 0
    source_ids = jnp.where(live_slots, slot_grid, 0)
    outgoing = (local_grad * factor)[source_ids]
    arrived = lax.all_to_all(outgoing, "shard", split_axis=0, concat_axis=2, tiled=True)[0]
    my_route = slot_grid[my_index]
    work_left, work_right = (left_held, right_held)

    def slot_work(slot_items):
        grad_block, left_mat, right_mat, is_live = slot_items

        def active(unused):
            left_new = beta_decay * left_mat + product(grad_block, grad_block.T)
            right_new = beta_decay * right_mat + product(grad_block.T, grad_block)
            return (precondition(grad_block, left_new, right_new), left_new, right_new)

        def vacant(unused):
            return (jnp.zeros_like(grad_block), left_mat, right_mat)

        return lax.cond(is_live, active, vacant, 0)

    precond, left_new, right_new = lax.map(
        slot_work, (arrived, work_left, work_right, my_route >= 0)
    )
    returned = lax.all_to_all(precond[None], "shard", split_axis=2, concat_axis=0, tiled=True)
    target = jnp.where(live_slots, slot_grid, block_count).reshape(-1)
    update = (
        jnp.zeros((block_count, row_count, width), jnp.float32)
        .at[target]
        .set(returned.reshape(-1, row_count, width), mode="drop")
    )
    new_left, new_right = (left_new, right_new)
    return (update[None], new_left[None], new_right[None])


def solution(mesh):
    placed = (
        P("expert", None, "shard", None),
        P("expert", "shard", None, None),
        P("expert", "shard", None, None),
        P("expert", None),
    )
    return jax.shard_map(
        body,
        mesh=mesh,
        in_specs=placed,
        out_specs=(
            P("expert", None, "shard", None),
            P("expert", "shard", None, None),
            P("expert", "shard", None, None),
        ),
        check_vma=False,
    )
```

profile of v0, /device:TPU:1, one launch (start us, length us, event | category | flops | bytes accessed | tf_op | source)
XLA Modules:
  0.0 321.3 jit_solution(18161480546851911121)
XLA Ops:
  0.6 0.0 copy-start.2
  0.6 2.1 multiply_reduce_fusion.3
  2.7 68.7 %psum.7 = f32[]{:T(128)} all-reduce(f32[]{:T(128)} %multiply_reduce_fusion.3), channel_id=1, replica_groups=mesh['expert'=4,'shard'=32] {'expert','shard'}, use_global_device_ids=true, to_apply=%region_1.0 | all-reduce | flops 1 | bytes 8 | tf_op jit(solution)/shard_map/psum | solution.py:48
  72.1 1.3 multiply_bitcast_fusion.1
  73.5 0.0 copy-done.2
  73.5 0.1 reshape_squeeze.9
  73.6 0.1 reshape.80
  73.7 2.4 gather_fusion
  76.1 5.0 %all-to-all-start = ((f32[32,3,16,512]{3,2,1,0:T(8,128)}), f32[32,3,16,512]{3,2,1,0:T(8,128)S(1)}, u32[]{:S(2)}, u32[]{:S(2)}) async-start(f32[32,3,16,512]{3,2,1,0:T(8,128)} %bitcast.73), calls=%async_computation | async-start | bytes 6291456 | tf_op jit(solution)/shard_map/all_to_all | solution.py:54
  81.1 0.5 broadcast.164
  81.6 0.7 reduce.6
  82.3 0.1 reshape_squeeze.8
  82.4 37.8 %all-to-all-done = f32[32,3,16,512]{3,2,1,0:T(8,128)S(1)} async-done(((f32[32,3,16,512]{3,2,1,0:T(8,128)}), f32[32,3,16,512]{3,2,1,0:T(8,128)S(1)}, u32[]{:S(2)}, u32[]{:S(2)}) %all-to-all-start) | async-done | bytes 3145760 | tf_op jit(solution)/shard_map/all_to_all | solution.py:54
  120.3 2.0 copy.22
  122.2 62.4 %while.14 = (s32[]{:T(128)}, f32[3,512,512]{2,1,0:T(8,128)}, f32[3,512,512]{2,1,0:T(8,128)}, f32[3,512,512]{2,1,0:T(8,128)}, pred[3]{0:T(512)(128)(4,1)S(1)}, /*...) while((s32[]{:T(128)}, f32[3,512,512]{2,1,0:T(8,128)}, ...), condition=%wide.region_9.10_spmd, body=%wide.region_2.9_spmd.sunk | while | flops 19339149312 | bytes 51383200 | solution.py:71
  122.2 1.3 dynamic-slice_bitcast_fusion.4
  123.5 1.3 dynamic-slice_bitcast_fusion.5
  124.8 0.6 dynamic_slice.46
  126.1 37.3 %conditional.2 = (f32[512,512]{1,0:T(8,128)S(1)}, f32[512,512]{1,0:T(8,128)S(1)}, f32[1,512,512]{2,1,0:T(8,128)}) conditional(s32[]{:T(128)} %bitcast.70, (f32[512,512]{1,0:T(8,128)S(1)}, f32[512,512]{1,0:T(8,128)S(1)}) %tuple.42, (f32[512,512]{1,0:T(8,128)S(1)}, f32[3,512,512]{2,1,0:T(8,128)}, s32[]{:T(128)}, f32[512,512]{1,0:T(8,128)S(1)}) %tuple.43), branch_computations={%region_3.3_spmd, %region_4.8_spmd} | conditional | flops 19339149312 | bytes 40896256 | solution.py:69
  126.1 4.4 %multiply_reduce_fusion.1 = (f32[]{:T(128)}, f32[512,512]{1,0:T(8,128)S(1)}) fusion(f32[3,512,512]{2,1,0:T(8,128)} %get-tuple-element.59, s32[]{:T(128)} %get-tuple-element.60, f32[512,512]{1,0:T(8,128)S(1)} %get-tuple-element.61), kind=kOutput, calls=%fused_computation.22 | convolution fusion | flops 1611661312 | bytes 3146244 | tf_op jit(solution)/shard_map/while/body/eval_jaxpr/cond/branch_1_fun/dot_general | solution.py:11
  131.2 2.0 fusion.16
  133.2 1.8 fusion.53
  135.0 1.9 fusion.1
  137.0 3.0 fusion.9
  140.0 4.7 %multiply_reduce_fusion.2 = (f32[]{:T(128)}, f32[512,512]{1,0:T(8,128)S(1)}) fusion(f32[3,512,512]{2,1,0:T(8,128)} %get-tuple-element.59, s32[]{:T(128)} %get-tuple-element.60, f32[512,512]{1,0:T(8,128)S(1)} %get-tuple-element.58), kind=kOutput, calls=%fused_computation.25 | convolution fusion | flops 1611661312 | bytes 3146244 | tf_op jit(solution)/shard_map/while/body/eval_jaxpr/cond/branch_1_fun/dot_general | solution.py:11
  145.3 2.0 fusion.19
  147.3 1.8 fusion.52
  149.1 1.9 fusion
  151.1 2.0 fusion.11
  153.1 0.0 copy-start
  153.1 3.2 fusion.4
  156.3 0.0 copy-done
  156.3 2.6 multiply_reduce_fusion
  159.6 2.1 fusion.8
  162.4 1.1 multiply_bitcast_fusion
  163.4 1.5 bitcast_dynamic-update-slice_fusion.3
  164.9 2.3 constant_dynamic-update-slice_fusion.2
  167.2 1.3 dynamic-slice_bitcast_fusion.4
  168.5 1.3 dynamic-slice_bitcast_fusion.5
  169.8 0.6 dynamic_slice.46
  171.0 1.1 conditional.2
  171.0 1.1 broadcast_in_dim.28
  172.1 1.5 bitcast_dynamic-update-slice_fusion.3
  173.6 2.3 constant_dynamic-update-slice_fusion.2
  175.9 1.3 dynamic-slice_bitcast_fusion.4
  177.2 1.3 dynamic-slice_bitcast_fusion.5
  178.5 0.6 dynamic_slice.46
  179.7 1.1 conditional.2
  179.7 1.1 broadcast_in_dim.28
  180.8 1.5 bitcast_dynamic-update-slice_fusion.3
  182.3 2.3 constant_dynamic-update-slice_fusion.2
  184.6 6.8 %copy.23 = f32[1,3,512,512]{3,0,1,2:T(1,128)} copy(f32[1,3,512,512]{3,2,1,0:T(8,128)} %bitcast.17) | data formatting | bytes 6291456 | tf_op jit(solution)/shard_map/broadcast_in_dim | solution.py:74
  191.4 77.5 %all-to-all-start.1 = ((f32[1,3,512,512]{3,0,1,2:T(1,128)}), f32[1,3,512,512]{3,0,1,2:T(1,128)S(1)}, u32[]{:S(2)}, u32[]{:S(2)}) async-start(f32[1,3,512,512]{3,0,1,2:T(1,128)} %copy.23), calls=%async_computation.1 | async-start | bytes 6291456 | tf_op jit(solution)/shard_map/all_to_all | solution.py:74
  268.9 39.2 %all-to-all-done.1 = f32[1,3,512,512]{3,0,1,2:T(1,128)S(1)} async-done(((f32[1,3,512,512]{3,0,1,2:T(1,128)}), f32[1,3,512,512]{3,0,1,2:T(1,128)S(1)}, u32[]{:S(2)}, u32[]{:S(2)}) %all-to-all-start.1) | async-done | bytes 3145760 | tf_op jit(solution)/shard_map/all_to_all | solution.py:74
  308.1 0.4 copy.24
  308.5 2.0 copy.25
  310.4 0.1 broadcast_in_dim.39
  310.6 9.7 %scatter_fusion = f32[32,16,512]{2,1,0:T(8,128)S(1)} fusion(f32[32,16,512]{2,1,0:T(8,128)S(1)} %broadcast_in_dim.39, s32[96]{0:T(128)S(1)} %fusion.51, f32[96,16,512]{2,1,0:T(8,128)} %bitcast.75), kind=kCustom, calls=%fused_computation.1 | custom fusion | bytes 9437568 | tf_op jit(solution)/shard_map/scatter | solution.py:79
  320.3 0.0 copy-start.1
  320.3 1.0 copy-done.1
  (7 shorter events, 0.0 us)
Async XLA Ops:
  0.6 72.8 %copy-start.2 = (s32[1,96]{1,0:T(1,128)S(1)}, s32[1,96]{1,0:T(1,128)}, u32[]{:S(2)}) copy-start(s32[1,96]{1,0:T(1,128)} %param.11) | copy-start | bytes 1156
  76.1 44.1 %all-to-all-start = ((f32[32,3,16,512]{3,2,1,0:T(8,128)}), f32[32,3,16,512]{3,2,1,0:T(8,128)S(1)}, u32[]{:S(2)}, u32[]{:S(2)}) async-start(f32[32,3,16,512]{3,2,1,0:T(8,128)} %bitcast.73), calls=%async_computation | async-start | bytes 6291456 | tf_op jit(solution)/shard_map/all_to_all | solution.py:54
  153.1 3.2 copy-start
  191.4 116.7 %all-to-all-start.1 = ((f32[1,3,512,512]{3,0,1,2:T(1,128)}), f32[1,3,512,512]{3,0,1,2:T(1,128)S(1)}, u32[]{:S(2)}, u32[]{:S(2)}) async-start(f32[1,3,512,512]{3,0,1,2:T(1,128)} %copy.23), calls=%async_computation.1 | async-start | bytes 6291456 | tf_op jit(solution)/shard_map/all_to_all | solution.py:74
  320.3 1.0 copy-start.1
where the time goes:
time: 324 us; the launch traced here: 321 us
  starting transfers between devices  82.4 us (25%)
  waiting for transfers between devices  77 us (24%)
  blocking collectives  68.7 us (21%)
  local copies, waits for them, and re-layouts  48.2 us (15%)
  matrix products  31.1 us (10%)
  other arithmetic  7.3 us (2%)
  loops' own time  5.05 us (2%)
    all_to_all x1, starting transfers between devices, body(): lax.all_to_all(precond[None], 'shard', split_axis=2, concat_axis=0, tiled...  77.5 us
    psum x1, blocking collectives, body(): total_sum = lax.psum(partial_sum, ('expert', 'shard'))  68.7 us
    all_to_all x1, waiting for transfers between devices, body(): lax.all_to_all(precond[None], 'shard', split_axis=2, concat_axis=0, tiled...  39.2 us
    all_to_all x1, waiting for transfers between devices, body(): lax.all_to_all(outgoing, 'shard', split_axis=0, concat_axis=2, tiled=True)  37.8 us
    dot_general x12, matrix products, product(): jnp.dot(left_mat, right_mat, precision=lax.Precision.HIGHEST, preferred_e...  31.1 us
    dynamic_update_slice x6, local copies, waits for them, and re-layouts, body(): lax.map(slot_work, (arrived, work_left, work_right, my_route >= 0))  11.3 us
    scatter x1, local copies, waits for them, and re-layouts, body(): update = jnp.zeros((block_count, row_count, width), jnp.float32).at[targe...  9.72 us
    squeeze x6, local copies, waits for them, and re-layouts, body(): lax.map(slot_work, (arrived, work_left, work_right, my_route >= 0))  7.78 us
  transfers between devices with their start and end apart: 2, of which 2 were waited for; matrix products, arithmetic and copies ran while one was open for 0% of the time, Pallas kernels for 0%

commit v1 on v0

v1 whole, which is shorter than its diff:
```python
import functools

import jax
import jax.numpy as jnp
from jax import lax
from jax.experimental import pallas as pl
from jax.experimental.pallas import tpu as pltpu
from jax.sharding import PartitionSpec as P

MESH = pl.DeviceIdType.MESH
F32 = jnp.float32
BF16 = jnp.bfloat16
NZ, NXC = 4, 8
HALF = 256

C0 = 25.0 / 16.0
C1 = -5.0 / 16.0 - 3125.0 / 4096.0
C2 = 3125.0 / 4096.0
C3 = -1250.0 / 4096.0
C4 = 250.0 / 4096.0
C5 = -25.0 / 4096.0
C6 = 1.0 / 4096.0


def split(value):
    high = value.astype(BF16)
    return high, (value - high.astype(F32)).astype(BF16)


def dot(a, b, dims=((1,), (0,))):
    return lax.dot_general(a, b, (dims, ((), ())), preferred_element_type=F32)


def total(value):
    return jnp.sum(jnp.sum(value, axis=1, keepdims=True), axis=0, keepdims=True)


def part(i):
    return pl.ds(i * HALF, HALF)


def body_kernel(
    assign_ref, slot_ref, grad_ref, left_ref, right_ref,
    update_ref, new_left_ref, new_right_ref,
    sent, m1, m2, held, back, n1, n2, returned,
    lbuf, rbuf, sums, sumv,
    sh, sl, a_buf, xh, xl, yh, yl, base, plh, pll, prh, prl,
    az_s, az_r, ax_s, ax_r, bz_s, bz_r, bx_s, bx_r, loc, sum_s, sum_r, io_in, io_out,
):
    e = lax.axis_index("expert")
    me = lax.axis_index("shard")
    z, xc = lax.div(me, NXC), lax.rem(me, NXC)

    def z_peer(d):
        return lax.rem(z + d, NZ)

    def xc_peer(d):
        return lax.rem(xc + d, NXC)

    barrier = pltpu.get_barrier_semaphore()
    for d in range(1, NZ):
        pl.semaphore_signal(barrier, inc=1, device_id=(e, z_peer(d) * NXC + xc), device_id_type=MESH)
        pl.semaphore_signal(barrier, inc=1, device_id=(lax.rem(e + d, 4), me), device_id_type=MESH)
    for d in range(1, NXC):
        pl.semaphore_signal(barrier, inc=1, device_id=(e, z * NXC + xc_peer(d)), device_id_type=MESH)

    loads = [
        pltpu.make_async_copy(left_ref.at[0], lbuf, io_in.at[0]),
        pltpu.make_async_copy(right_ref.at[0], rbuf, io_in.at[1]),
    ]
    for copy in loads:
        copy.start()

    def square_sum(b, acc):
        rows = grad_ref[0, b]
        sq = rows * rows
        for c in range(4):
            acc = acc + sq[0:8, c * 128:(c + 1) * 128] + sq[8:16, c * 128:(c + 1) * 128]
        return acc

    sums[0] = lax.fori_loop(0, grad_ref.shape[1], square_sum, jnp.zeros((8, 128), F32))

    def build(k):
        def one(d, carry):
            block = jnp.maximum(assign_ref[0, d * 3 + k], 0)
            sent[k, lax.div(d, NXC), lax.rem(d, NXC)] = grad_ref[0, block].reshape(2, 8, 512)
            return carry

        lax.fori_loop(0, NZ * NXC, one, 0)

    def a_copies(src, mid1, mid2, k, r):
        out = []
        for d in (1, 3, 2):
            t = z_peer(d)
            out.append(pltpu.make_async_remote_copy(
                src_ref=src.at[k, t, :, 0], dst_ref=mid1.at[k, z],
                send_sem=az_s.at[r, d - 1], recv_sem=az_r.at[r, d - 1],
                device_id=(e, t * NXC + xc), device_id_type=MESH))
        for d in (1, 7, 2, 6, 3, 5, 4):
            t = xc_peer(d)
            out.append(pltpu.make_async_remote_copy(
                src_ref=src.at[k, :, t, 1], dst_ref=mid2.at[k, xc],
                send_sem=ax_s.at[r, d - 1], recv_sem=ax_r.at[r, d - 1],
                device_id=(e, z * NXC + t), device_id_type=MESH))
        out.append(pltpu.make_async_copy(src.at[k, z, :, 0], mid1.at[k, z], loc.at[r, 0]))
        out.append(pltpu.make_async_copy(src.at[k, :, xc, 1], mid2.at[k, xc], loc.at[r, 1]))
        return out

    def b_copies(mid1, mid2, dst, k, r):
        out = []
        for d in (1, 7, 2, 6, 3, 5, 4):
            t = xc_peer(d)
            out.append(pltpu.make_async_remote_copy(
                src_ref=mid1.at[k, :, t], dst_ref=dst.at[k, :, xc, 0],
                send_sem=bx_s.at[r, d - 1], recv_sem=bx_r.at[r, d - 1],
                device_id=(e, z * NXC + t), device_id_type=MESH))
        for d in (1, 3, 2):
            t = z_peer(d)
            out.append(pltpu.make_async_remote_copy(
                src_ref=mid2.at[k, :, t], dst_ref=dst.at[k, z, :, 1],
                send_sem=bz_s.at[r, d - 1], recv_sem=bz_r.at[r, d - 1],
                device_id=(e, t * NXC + xc), device_id_type=MESH))
        out.append(pltpu.make_async_copy(mid1.at[k, :, xc], dst.at[k, :, xc, 0], loc.at[r, 2]))
        out.append(pltpu.make_async_copy(mid2.at[k, :, z], dst.at[k, z, :, 1], loc.at[r, 3]))
        return out

    def start(copies):
        for copy in copies:
            copy.start()

    def landed(copies):
        for copy in copies[:-2]:
            copy.wait_recv()
        for copy in copies[-2:]:
            copy.wait()

    def left_here(copies):
        for copy in copies[:-2]:
            copy.wait_send()

    fwd_a = lambda k: a_copies(sent, m1, m2, k, k)
    fwd_b = lambda k: b_copies(m1, m2, held, k, k)
    ret_a = lambda k: a_copies(back, n1, n2, k, 3 + k)
    ret_b = lambda k: b_copies(n1, n2, returned, k, 3 + k)

    build(0)
    pl.semaphore_wait(barrier, 2 * (NZ - 1) + NXC - 1)

    sum_copies = []

    def sum_stage(stage, first, peers):
        copies = []
        for i, peer in enumerate(peers):
            copies.append(pltpu.make_async_remote_copy(
                src_ref=sums.at[stage], dst_ref=sumv.at[first + i],
                send_sem=sum_s.at[first + i], recv_sem=sum_r.at[first + i],
                device_id=peer, device_id_type=MESH))
        start(copies)
        sum_copies.extend(copies)
        return copies

    def sum_take(stage, first, copies):
        acc = sums[stage]
        for i, copy in enumerate(copies):
            copy.wait_recv()
            acc = acc + sumv[first + i]
        sums[stage + 1] = acc

    s0 = sum_stage(0, 0, [(lax.rem(e + d, 4), me) for d in range(1, 4)])
    start(fwd_a(0))
    build(1)
    start(fwd_a(1))
    sum_take(0, 0, s0)
    s1 = sum_stage(1, 3, [(e, z_peer(d) * NXC + xc) for d in range(1, NZ)])
    build(2)
    sum_take(1, 3, s1)
    s2 = sum_stage(2, 6, [(e, z * NXC + xc_peer(d)) for d in range(1, NXC)])
    landed(fwd_a(0))
    start(fwd_b(0))
    sum_take(2, 6, s2)
    entries = 4.0 * 32.0 * 512.0 * 512.0
    mean_square = total(sums[3]) / entries
    factor = jnp.minimum(1.0, 1.0 / jnp.sqrt(mean_square + 1e-06))
    landed(fwd_a(1))
    start(fwd_b(1))
    start(fwd_a(2))
    for copy in loads:
        copy.wait()

    def put(high, low, i, j, value):
        a, b = split(value)
        high[part(i), part(j)] = a
        low[part(i), part(j)] = b

    def root(square, oh, ol):
        norm = jnp.sqrt(square + 1e-06)
        inverse = 1.0 / norm
        for i in range(2):
            for j in range(2):
                put(xh, xl, i, j, a_buf[part(i), part(j)] * inverse)
        for i, j in ((0, 0), (0, 1), (1, 1)):
            low = dot(xh[part(i), :], xl[:, part(j)])
            other = low if i == j else dot(xh[part(j), :], xl[:, part(i)])
            value = dot(xh[part(i), :], xh[:, part(j)]) + (low + other.T)
            put(yh, yl, i, j, value)
            base[part(i), part(j)] = value
            if i != j:
                put(yh, yl, j, i, value.T)
        cubes = {}
        for i, j in ((0, 0), (0, 1), (1, 1)):
            cubes[i, j] = (
                dot(yh[part(i), :], xh[:, part(j)])
                + (dot(yh[part(i), :], xl[:, part(j)]) + dot(yl[part(i), :], xh[:, part(j)]))
            )
            x1 = a_buf[part(i), part(j)] * inverse
            x2 = base[part(i), part(j)]
            x3 = cubes[i, j]
            value = C1 * x1 + C2 * x2 + C3 * x3
            if i == j:
                rows = lax.broadcasted_iota(jnp.int32, (HALF, HALF), 0)
                cols = lax.broadcasted_iota(jnp.int32, (HALF, HALF), 1)
                value = value + jnp.where(rows == cols, C0, 0.0)
            base[part(i), part(j)] = value
            a_buf[part(i), part(j)] = C4 * x1 + C5 * x2 + C6 * x3
            cubes[i, j] = None
            put(oh, ol, i, j, x3)
            if i != j:
                put(oh, ol, j, i, x3.T)
        for i, j in ((0, 0), (0, 1), (1, 1)):
            put(xh, xl, i, j, a_buf[part(i), part(j)])
            if i != j:
                put(xh, xl, j, i, a_buf[part(i), part(j)].T)
        for i, j in ((0, 0), (0, 1), (1, 1)):
            base[part(i), part(j)] += (
                dot(oh[part(i), :], xh[:, part(j)])
                + (dot(oh[part(i), :], xl[:, part(j)]) + dot(ol[part(i), :], xh[:, part(j)]))
            )
        for i, j in ((0, 0), (0, 1), (1, 1)):
            value = base[part(i), part(j)]
            put(oh, ol, i, j, value)
            if i != j:
                put(oh, ol, j, i, value.T)
        return jnp.sqrt(jnp.sqrt(norm))

    def stat(buf, k, live, products):
        square = jnp.zeros((1, 1), F32)
        for i in range(2):
            for j in range(2):
                old = buf[k, part(i), part(j)]
                new = 0.95 * old + products(i, j)
                a_buf[part(i), part(j)] = new
                square = square + total(new * new)
                buf[k, part(i), part(j)] = jnp.where(live, new, old)
        return square

    def slot(k):
        live = assign_ref[0, me * 3 + k] >= 0
        graft = jnp.zeros((1, 1), F32)
        for i in range(2):
            for j in range(2):
                piece = held[k, 2 * i:2 * i + 2, :, :, :, part(j)].reshape(HALF, HALF) * factor
                graft = graft + total(piece * piece)
                put(sh, sl, i, j, piece)

        def left_product(i, j):
            rows, cols = part(i), part(j)
            nt = ((1,), (1,))
            return dot(sh[rows, :], sh[cols, :], nt) + (
                dot(sh[rows, :], sl[cols, :], nt) + dot(sl[rows, :], sh[cols, :], nt))

        def right_product(i, j):
            rows, cols = part(i), part(j)
            tn = ((0,), (0,))
            return dot(sh[:, rows], sh[:, cols], tn) + (
                dot(sh[:, rows], sl[:, cols], tn) + dot(sl[:, rows], sh[:, cols], tn))

        left_scale = root(stat(lbuf, k, live, left_product), plh, pll)
        pltpu.make_async_copy(lbuf.at[k], new_left_ref.at[0, k], io_out.at[0, k]).start()
        right_scale = root(stat(rbuf, k, live, right_product), prh, prl)
        pltpu.make_async_copy(rbuf.at[k], new_right_ref.at[0, k], io_out.at[1, k]).start()

        for i in range(2):
            for j in range(2):
                put(xh, xl, i, j, dot(plh[part(i), :], sh[:, part(j)])
                    + (dot(plh[part(i), :], sl[:, part(j)]) + dot(pll[part(i), :], sh[:, part(j)])))
        square = jnp.zeros((1, 1), F32)
        scale = 1.0 / (left_scale * right_scale)
        for i in range(2):
            for j in range(2):
                value = dot(xh[part(i), :], prh[:, part(j)]) + (
                    dot(xh[part(i), :], prl[:, part(j)]) + dot(xl[part(i), :], prh[:, part(j)]))
                value = value * scale
                square = square + total(value * value)
                a_buf[part(i), part(j)] = value
        count = 512.0 * 512.0
        ratio = jnp.sqrt(graft / count + 1e-12) / jnp.sqrt(square / count + 1e-12)
        for i in range(2):
            back[k, 2 * i:2 * i + 2] = (a_buf[part(i), :] * ratio).reshape(2, NXC, 2, 8, 512)

    def turn(k, carry):
        landed(fwd_b(k))
        slot(k)
        start(ret_a(k))

        @pl.when(k == 0)
        def _():
            landed(fwd_a(2))
            start(fwd_b(2))

        @pl.when(k > 0)
        def _():
            landed(ret_a(k - 1))
            start(ret_b(k - 1))

        return carry

    lax.fori_loop(0, 3, turn, 0)
    landed(ret_a(2))
    start(ret_b(2))
    for k in range(3):
        left_here(fwd_a(k))
        left_here(fwd_b(k))
        left_here(ret_a(k))
    for copy in sum_copies:
        copy.wait_send()
    for k in range(3):
        pltpu.make_async_copy(lbuf.at[k], new_left_ref.at[0, k], io_out.at[0, k]).wait()
        pltpu.make_async_copy(rbuf.at[k], new_right_ref.at[0, k], io_out.at[1, k]).wait()
    for k in range(3):
        landed(ret_b(k))
        left_here(ret_b(k))

    def take(b, carry):
        s = slot_ref[0, b]
        d, k = lax.div(s, 3), lax.rem(s, 3)
        update_ref[0, b] = returned[k, lax.div(d, NXC), lax.rem(d, NXC)].reshape(16, 512)
        return carry

    lax.fori_loop(0, update_ref.shape[1], take, 0)


def body(gradient, left_stat, right_stat, assign):
    ids = jnp.arange(32, dtype=jnp.int32)
    slots = jnp.arange(96, dtype=jnp.int32)
    slot_of = jnp.sum(jnp.where(assign[0][None, :] == ids[:, None], slots[None, :], 0), axis=1).astype(jnp.int32)
    piece = (3, NZ, NXC, 2, 8, 512)
    vm = lambda shape, dtype=F32: pltpu.VMEM(shape, dtype)
    dma = lambda *shape: pltpu.SemaphoreType.DMA(shape)
    mat = (512, 512)
    any_spec = pl.BlockSpec(memory_space=pl.ANY)
    return pl.pallas_call(
        body_kernel,
        out_shape=(
            jax.ShapeDtypeStruct(gradient.shape, F32),
            jax.ShapeDtypeStruct(left_stat.shape, F32),
            jax.ShapeDtypeStruct(right_stat.shape, F32),
        ),
        in_specs=[
            pl.BlockSpec(memory_space=pltpu.SMEM),
            pl.BlockSpec(memory_space=pltpu.SMEM),
            pl.BlockSpec(memory_space=pltpu.VMEM),
            any_spec, any_spec,
        ],
        out_specs=(pl.BlockSpec(memory_space=pltpu.VMEM), any_spec, any_spec),
        scratch_shapes=[
            vm(piece), vm((3, NZ, NXC, 8, 512)), vm((3, NXC, NZ, 8, 512)), vm(piece),
            vm(piece), vm((3, NZ, NXC, 8, 512)), vm((3, NXC, NZ, 8, 512)), vm(piece),
            vm((3,) + mat), vm((3,) + mat), vm((4, 8, 128)), vm((13, 8, 128)),
            vm(mat, BF16), vm(mat, BF16), vm(mat), vm(mat, BF16), vm(mat, BF16), vm(mat, BF16), vm(mat, BF16), vm(mat),
            vm(mat, BF16), vm(mat, BF16), vm(mat, BF16), vm(mat, BF16),
            dma(6, 3), dma(6, 3), dma(6, 7), dma(6, 7), dma(6, 3), dma(6, 3), dma(6, 7), dma(6, 7),
            dma(6, 4), dma(13), dma(13), dma(2), dma(2, 3),
        ],
        name="shampoo",
        compiler_params=pltpu.CompilerParams(collective_id=0, has_side_effects=True, vmem_limit_bytes=58 * 2**20),
    )(assign, slot_of[None], gradient, left_stat, right_stat)


def solution(mesh):
    placed = P("expert", None, "shard", None)
    slots = P("expert", "shard", None, None)
    return jax.shard_map(
        body,
        mesh=mesh,
        in_specs=(placed, slots, slots, P("expert", None)),
        out_specs=(placed, slots, slots),
        check_vma=False,
    )
```

time: 324 us -> 94.3 us (0.29)
  Pallas kernels: 0 us -> 84.2 us
  starting transfers between devices: 82.4 us -> 0 us
  waiting for transfers between devices: 77 us -> 0 us
  blocking collectives: 68.7 us -> 0 us
  local copies, waits for them, and re-layouts: 48.2 us -> 7.99 us
  matrix products: 31.1 us -> 0 us
  other arithmetic: 7.3 us -> 1.28 us
  loops' own time: 5.05 us -> 0 us
    pallas_call x0 -> x1, Pallas kernels: none -> 84.2 us  [body(): pl.pallas_call(body_kernel, out_shape=(jax.ShapeDtypeStruct(gradient.shap...]
    all_to_all x2 -> x0, starting transfers between devices: 82.4 us -> none  [the longest x1 77.5 us: body(): lax.all_to_all(precond[None], 'shard', split_axis=2, concat_axis=0, tiled...]
    all_to_all x2 -> x0, waiting for transfers between devices: 77 us -> none  [the longest x1 39.2 us: body(): lax.all_to_all(precond[None], 'shard', split_axis=2, concat_axis=0, tiled...]
    psum x1 -> x0, blocking collectives: 68.7 us -> none  [body(): total_sum = lax.psum(partial_sum, ('expert', 'shard'))]
    dot_general x12 -> x0, matrix products: 31.1 us -> none  [product(): jnp.dot(left_mat, right_mat, precision=lax.Precision.HIGHEST, preferred_e...]
    dynamic_update_slice x6 -> x0, local copies, waits for them, and re-layouts: 11.3 us -> none  [body(): lax.map(slot_work, (arrived, work_left, work_right, my_route >= 0))]
    scatter x1 -> x0, local copies, waits for them, and re-layouts: 9.72 us -> none  [body(): update = jnp.zeros((block_count, row_count, width), jnp.float32).at[targe...]
    broadcast_in_dim x4 -> x0, local copies, waits for them, and re-layouts: 9.1 us -> none  [the longest x1 6.79 us: body(): precond[None]]
  transfers between devices with their start and end apart: 2 -> 0, of which waited for: 2 -> 0; matrix products, arithmetic and copies ran while one was open for 0% -> 0% of each run, Pallas kernels for 0% -> 0%
where the time goes in v1:
time: 94.3 us; the launch traced here: 94.1 us
  Pallas kernels  84.2 us (89%)
  local copies, waits for them, and re-layouts  7.99 us (8%)
  other arithmetic  1.28 us (1%)
    pallas_call x1, Pallas kernels, body(): pl.pallas_call(body_kernel, out_shape=(jax.ShapeDtypeStruct(gradient.shap...  84.2 us
    unnamed x5, local copies, waits for them, and re-layouts  7.99 us

profile of v1, /device:TPU:1, one launch (start us, length us, event | category | flops | bytes accessed | tf_op | source)
XLA Modules:
  0.0 94.1 jit_solution(13380651146372551198)
XLA Ops:
  0.6 1.3 %select_reduce_fusion = s32[32]{0:T(128)} fusion(s32[96]{0:T(128)} %bitcast.2), kind=kLoop, calls=%fused_computation | loop fusion | flops 9184 | bytes 512 | tf_op jit(solution)/shard_map/reduce_sum | solution.py:345
  1.9 84.2 %shampoo.1 = (f32[1,32,16,512]{3,2,1,0:T(8,128)}, f32[1,3,512,512]{3,2,1,0:T(8,128)}, f32[1,3,512,512]{3,2,1,0:T(8,128)}) custom-call(s32[1,96]{1,0:T(1,128)} %assign_ref.1, s32[1,32]{1,0:T(1,128)} %bitcast.3, f32[1,32,16,512]{3,2,1,0:T(8,128)} %grad_ref.1, f32[1,3,512,512]{3,2,1,0:T(8,128)} %left_ref.1, f32[1,3,512,512]{3,2,1,0:T(8,128)} %right_ref.1), custom_call_target="tpu_custom_call" | custom-call | tf_op jit(solution)/shard_map/shampoo/pallas_call | solution.py:351
  86.1 2.3 %copy.10 = f32[1,32,16,512]{3,2,1,0:T(8,128)} copy(f32[1,32,16,512]{3,2,1,0:T(8,128)} %get-tuple-element.6) | data formatting | bytes 2097152
  88.4 0.0 copy-start
  88.4 4.0 %copy.11 = f32[1,3,512,512]{3,2,1,0:T(8,128)} copy(f32[1,3,512,512]{3,2,1,0:T(8,128)} %get-tuple-element.7) | data formatting | bytes 6291456
  92.4 0.0 copy-done
  92.4 1.7 %copy.12 = f32[1,3,512,512]{3,2,1,0:T(8,128)} copy(f32[1,3,512,512]{3,2,1,0:T(8,128)S(1)} %copy-done) | data formatting | bytes 6291456
Async XLA Ops:
  88.4 4.0 %copy-start = (f32[1,3,512,512]{3,2,1,0:T(8,128)S(1)}, f32[1,3,512,512]{3,2,1,0:T(8,128)}, u32[]{:S(2)}) copy-start(f32[1,3,512,512]{3,2,1,0:T(8,128)} %get-tuple-element.8) | copy-start | bytes 9437188

commit v2 on v1

v2 whole, which is shorter than its diff:
```python
import functools

import jax
import jax.numpy as jnp
from jax import lax
from jax.experimental import pallas as pl
from jax.experimental.pallas import tpu as pltpu
from jax.sharding import PartitionSpec as P

MESH = pl.DeviceIdType.MESH
F32 = jnp.float32
BF16 = jnp.bfloat16
HALF = 256
CAP = 8
FULL = 16
LIST_A, LIST_B, OWNER, ENTRY_A, ENTRY_B, OVER = range(6)

C0 = 25.0 / 16.0
C1 = -5.0 / 16.0 - 3125.0 / 4096.0
C2 = 3125.0 / 4096.0
C3 = -1250.0 / 4096.0
C4 = 250.0 / 4096.0
C5 = -25.0 / 4096.0
C6 = 1.0 / 4096.0


def split(value):
    high = value.astype(BF16)
    return high, (value - high.astype(F32)).astype(BF16)


def dot(a, b, dims=((1,), (0,))):
    return lax.dot_general(a, b, (dims, ((), ())), preferred_element_type=F32)


def total(value):
    return jnp.sum(jnp.sum(value, axis=1, keepdims=True), axis=0, keepdims=True)


def part(i):
    return pl.ds(i * HALF, HALF)


def place(slot):
    d = (slot * 43) >> 7
    z, x, c = d >> 3, (d >> 1) & 3, d & 1
    return slot - 3 * d, z, x, d & 7, z * 2 + c


def table_kernel(assign_ref, table_ref, row):
    shape = (128, 128)
    row[...] = jnp.full((8, 128), -1.0, F32)
    row[0:1, 0:96] = assign_ref[...].astype(F32)
    across = jnp.broadcast_to(row[0:1, :], shape)
    down = across.T
    i = lax.broadcasted_iota(jnp.int32, shape, 0)
    j = lax.broadcasted_iota(jnp.int32, shape, 1)
    rank_i, za_i, xa_i, _, _ = place(i)
    rank_j, za_j, xa_j, b0_j, b1_j = place(j)
    more_i = (down >= 0.0) & (rank_i > 0)
    more_j = (across >= 0.0) & (rank_j > 0)

    def count(mask, axis):
        return jnp.sum(jnp.where(mask, 1.0, 0.0), axis=axis, keepdims=True)

    over = jnp.zeros((1, 1), F32)
    for h, (ga_i, ga_j, b_j) in enumerate(((za_i, za_j, b0_j), (xa_i, xa_j, b1_j))):
        same = ga_i == ga_j
        before_i = count(more_j & same & (j < i), 1)
        before_j = count(more_i & same & (i < j), 0)
        listed = more_i & (ga_i == (j >> 4)) & (before_i == (j & 15).astype(F32))
        spots = jnp.sum(jnp.where(listed, i.astype(F32), 0.0), axis=0, keepdims=True)
        table_ref[LIST_A + h:LIST_A + h + 1, :] = spots.astype(jnp.int32)
        entry = jnp.where(rank_j[0:1] == 0, b_j[0:1].astype(F32), 8.0 + before_j)
        table_ref[ENTRY_A + h:ENTRY_A + h + 1, :] = entry.astype(jnp.int32)
        over = over + count(more_j[0:1] & (before_j >= float(CAP)), 1)
    owner = jnp.sum(jnp.where(down == j.astype(F32), i.astype(F32), 0.0), axis=0, keepdims=True)
    table_ref[OWNER:OWNER + 1, :] = owner.astype(jnp.int32)
    table_ref[OVER:OVER + 1, :] = jnp.broadcast_to(over, (1, 128)).astype(jnp.int32)
    table_ref[OVER + 1:8, :] = jnp.zeros((7 - OVER, 128), jnp.int32)


def step_kernel(
    cap,
    assign_ref, table_ref, grad_ref, left_ref, right_ref,
    update_ref, new_left_ref, new_right_ref, over_ref,
    sent, mid, pad, held, back, rmid, comp, fin,
    lbuf, rbuf, sums, sumv,
    sh, sl, a_buf, xh, xl, yh, yl, base, plh, pll, prh, prl,
    a_s, a_r, b_s, b_r, loc, sum_s, sum_r, io_in, io_out,
):
    e = lax.axis_index("expert")
    me = lax.axis_index("shard")
    z, x, c = lax.div(me, 8), lax.rem(lax.div(me, 2), 4), lax.rem(me, 2)
    group = (z, x)
    spot = (x * 2 + c, z * 2 + c)

    def device(h, a, b):
        if h == 0:
            return (e, a * 8 + b)
        return (e, lax.div(b, 2) * 8 + a * 2 + lax.rem(b, 2))

    def index(h, a, b):
        return device(h, a, b)[1]

    barrier = pltpu.get_barrier_semaphore()
    for d in range(1, 4):
        pl.semaphore_signal(barrier, inc=1, device_id=(lax.rem(e + d, 4), me), device_id_type=MESH)
    for d in range(1, 8):
        pl.semaphore_signal(barrier, inc=1, device_id=device(0, z, lax.rem(spot[0] + d, 8)), device_id_type=MESH)
    for d in range(1, 4):
        for f in range(2):
            pl.semaphore_signal(
                barrier, inc=1, device_id=(e, lax.rem(z + d, 4) * 8 + x * 2 + lax.rem(c + f, 2)), device_id_type=MESH)

    loads = [
        pltpu.make_async_copy(left_ref.at[0], lbuf, io_in.at[0]),
        pltpu.make_async_copy(right_ref.at[0], rbuf, io_in.at[1]),
    ]
    for copy in loads:
        copy.start()

    def square_sum(b, acc):
        rows = grad_ref[0, b]
        sq = rows * rows
        for q in range(4):
            acc = acc + sq[0:8, q * 128:(q + 1) * 128] + sq[8:16, q * 128:(q + 1) * 128]
        return acc

    sums[0, 0] = lax.fori_loop(0, grad_ref.shape[1], square_sum, jnp.zeros((8, 128), F32))
    sums[0, 1] = jnp.full((8, 128), table_ref[OVER, 0].astype(F32), F32)

    def build_first(d, carry):
        block = jnp.maximum(assign_ref[0, d * 3], 0)
        rows = grad_ref[0, block]
        zd, xd, cd = lax.div(d, 8), lax.rem(lax.div(d, 2), 4), lax.rem(d, 2)
        sent[0, zd, xd * 2 + cd] = rows[0:8]
        sent[1, xd, zd * 2 + cd] = rows[8:16]
        return carry

    def build_more(n, carry):
        a, j = lax.div(n, cap), lax.rem(n, cap)
        for h in range(2):
            block = jnp.maximum(assign_ref[0, table_ref[LIST_A + h, a * 16 + j]], 0)
            sent[h, a, 8 + j] = grad_ref[0, block, h * 8:h * 8 + 8]
        return carry

    def build_pad(k):
        def one(b, carry):
            for h in range(2):
                entry = jnp.minimum(table_ref[ENTRY_A + h, index(h, group[h], b) * 3 + k], 7 + cap)
                pad[k - 1, h, b] = mid[h, :, entry]
            return carry

        lax.fori_loop(0, 8, one, 0)

    def build_comp(j, carry):
        for h in range(2):
            rank, _, _, b0, b1 = place(table_ref[LIST_A + h, group[h] * 16 + j])
            comp[h, :, j] = rmid[rank, h, (b0, b1)[h]]
        return carry

    first, more = pl.ds(0, 8), pl.ds(8, cap)
    near, ring = (1, 3, 2), (1, 7, 2, 6, 3, 5, 4)

    def along(r, src, dst):
        out, here = [], []
        for d in near:
            for h in range(2):
                t = lax.rem(group[h] + d, 4)
                out.append(pltpu.make_async_remote_copy(
                    src_ref=src(h, t), dst_ref=dst(h, group[h]),
                    send_sem=a_s.at[r, h, d - 1], recv_sem=a_r.at[r, h, d - 1],
                    device_id=device(h, t, spot[h]), device_id_type=MESH))
        for h in range(2):
            here.append(pltpu.make_async_copy(src(h, group[h]), dst(h, group[h]), loc.at[r, h]))
        return out, here

    def within(r, src, dst):
        out, here = [], []
        for d in ring:
            for h in range(2):
                t = lax.rem(spot[h] + d, 8)
                out.append(pltpu.make_async_remote_copy(
                    src_ref=src(h, t), dst_ref=dst(h, spot[h]),
                    send_sem=b_s.at[r, h, d - 1], recv_sem=b_r.at[r, h, d - 1],
                    device_id=device(h, group[h], t), device_id_type=MESH))
        for h in range(2):
            here.append(pltpu.make_async_copy(src(h, spot[h]), dst(h, spot[h]), loc.at[4 + r, h]))
        return out, here

    def rows_of(ref, k):
        def pick(h, b):
            if h == 0:
                return ref.at[k, :, lax.div(b, 2), lax.rem(b, 2), 0]
            return ref.at[k, lax.div(b, 2), :, lax.rem(b, 2), 1]

        return pick

    out_first = lambda: along(0, lambda h, a: sent.at[h, a, first], lambda h, a: mid.at[h, a, first])
    out_more = lambda: along(1, lambda h, a: sent.at[h, a, more], lambda h, a: mid.at[h, a, more])
    to_first = lambda: within(0, lambda h, b: mid.at[h, :, b], rows_of(held, 0))
    to_more = lambda k: within(k, lambda h, b: pad.at[k - 1, h, b], rows_of(held, k))
    arrive = lambda k: within(k, lambda h, b: pad.at[0, h, b], rows_of(held, k))
    from_slot = lambda k: within(3 + k, rows_of(back, k), lambda h, b: rmid.at[k, h, b])
    in_first = lambda: along(2, lambda h, a: rmid.at[0, h, :, a], lambda h, a: fin.at[h, a, first])
    in_more = lambda: along(3, lambda h, a: comp.at[h, a], lambda h, a: fin.at[h, a, more])

    def start(copies):
        for copy in copies[0] + copies[1]:
            copy.start()

    def landed(copies):
        for copy in copies[0]:
            copy.wait_recv()
        for copy in copies[1]:
            copy.wait()

    def gone(copies):
        for copy in copies[0]:
            copy.wait_send()

    lax.fori_loop(0, 32, build_first, 0)
    pl.semaphore_wait(barrier, 16)

    sum_copies = []

    def sum_stage(stage, at, peers):
        copies = []
        for i, peer in enumerate(peers):
            copies.append(pltpu.make_async_remote_copy(
                src_ref=sums.at[stage], dst_ref=sumv.at[at + i],
                send_sem=sum_s.at[at + i], recv_sem=sum_r.at[at + i],
                device_id=peer, device_id_type=MESH))
        for copy in copies:
            copy.start()
        sum_copies.extend(copies)
        return copies

    def sum_take(stage, at, copies):
        acc = sums[stage]
        for i, copy in enumerate(copies):
            copy.wait_recv()
            acc = acc + sumv[at + i]
        sums[stage + 1] = acc

    s0 = sum_stage(0, 0, [(lax.rem(e + d, 4), me) for d in range(1, 4)])
    start(out_first())
    lax.fori_loop(0, 4 * cap, build_more, 0)
    start(out_more())
    sum_take(0, 0, s0)
    s1 = sum_stage(1, 3, [device(0, lax.rem(z + d, 4), spot[0]) for d in range(1, 4)])
    sum_take(1, 3, s1)
    s2 = sum_stage(2, 6, [device(0, z, lax.rem(spot[0] + d, 8)) for d in range(1, 8)])
    landed(out_first())
    start(to_first())
    sum_take(2, 6, s2)
    mean_square = total(sums[3, 0]) / (4.0 * 32.0 * 512.0 * 512.0)
    factor = jnp.minimum(1.0, 1.0 / jnp.sqrt(mean_square + 1e-06))
    over_ref[...] = sums[3, 1]
    landed(out_more())
    build_pad(1)
    start(to_more(1))
    build_pad(2)
    start(to_more(2))
    for copy in loads:
        copy.wait()

    def put(high, low, i, j, value):
        a, b = split(value)
        high[part(i), part(j)] = a
        low[part(i), part(j)] = b

    def both(high, low, i, j, value):
        put(high, low, i, j, value)
        if i != j:
            put(high, low, j, i, value.T)

    tiles = ((0, 0), (0, 1), (1, 1))

    def root(square, oh, ol):
        norm = jnp.sqrt(square + 1e-06)
        inverse = 1.0 / norm
        for i in range(2):
            for j in range(2):
                put(xh, xl, i, j, a_buf[part(i), part(j)] * inverse)
        for i, j in tiles:
            low = dot(xh[part(i), :], xl[:, part(j)])
            other = low if i == j else dot(xh[part(j), :], xl[:, part(i)])
            value = dot(xh[part(i), :], xh[:, part(j)]) + (low + other.T)
            both(yh, yl, i, j, value)
            base[part(i), part(j)] = value
        for i, j in tiles:
            x3 = (
                dot(yh[part(i), :], xh[:, part(j)])
                + (dot(yh[part(i), :], xl[:, part(j)]) + dot(yl[part(i), :], xh[:, part(j)]))
            )
            x1 = a_buf[part(i), part(j)] * inverse
            x2 = base[part(i), part(j)]
            value = C1 * x1 + C2 * x2 + C3 * x3
            if i == j:
                rows = lax.broadcasted_iota(jnp.int32, (HALF, HALF), 0)
                cols = lax.broadcasted_iota(jnp.int32, (HALF, HALF), 1)
                value = value + jnp.where(rows == cols, C0, 0.0)
            base[part(i), part(j)] = value
            high = x3.astype(BF16)
            rest = (C4 * x1 + C5 * x2 + C6 * x3)
            oh[part(i), part(j)] = high
            ol[part(i), part(j)] = rest.astype(BF16)
            if i != j:
                oh[part(j), part(i)] = x3.T.astype(BF16)
                ol[part(j), part(i)] = rest.T.astype(BF16)
        for i, j in tiles:
            base[part(i), part(j)] += dot(oh[part(i), :], ol[:, part(j)])
        for i, j in tiles:
            both(oh, ol, i, j, base[part(i), part(j)])
        return jnp.sqrt(jnp.sqrt(norm))

    def stat(buf, k, live, high, low):
        square = jnp.zeros((1, 1), F32)

        def take(i, j, product):
            old = buf[k, part(i), part(j)]
            new = 0.95 * old + product
            a_buf[part(i), part(j)] = new
            buf[k, part(i), part(j)] = jnp.where(live, new, old)
            return total(new * new)

        for i, j in tiles:
            one = low(i, j)
            other = one if i == j else low(j, i)
            product = high(i, j) + (one + other.T)
            square = square + take(i, j, product)
            if i != j:
                square = square + take(j, i, product.T)
        return square

    def slot(k):
        live = assign_ref[0, me * 3 + k] >= 0
        graft = jnp.zeros((1, 1), F32)
        for i in range(2):
            for j in range(2):
                piece = held[k, 2 * i:2 * i + 2, :, :, :, :, part(j)].reshape(HALF, HALF) * factor
                graft = graft + total(piece * piece)
                put(sh, sl, i, j, piece)
        nt, tn = ((1,), (1,)), ((0,), (0,))
        left_scale = root(stat(
            lbuf, k, live,
            lambda i, j: dot(sh[part(i), :], sh[part(j), :], nt),
            lambda i, j: dot(sh[part(i), :], sl[part(j), :], nt)), plh, pll)
        pltpu.make_async_copy(lbuf.at[k], new_left_ref.at[0, k], io_out.at[0, k]).start()
        right_scale = root(stat(
            rbuf, k, live,
            lambda i, j: dot(sh[:, part(i)], sh[:, part(j)], tn),
            lambda i, j: dot(sh[:, part(i)], sl[:, part(j)], tn)), prh, prl)
        pltpu.make_async_copy(rbuf.at[k], new_right_ref.at[0, k], io_out.at[1, k]).start()

        for i in range(2):
            for j in range(2):
                put(xh, xl, i, j, dot(plh[part(i), :], sh[:, part(j)])
                    + (dot(plh[part(i), :], sl[:, part(j)]) + dot(pll[part(i), :], sh[:, part(j)])))
        square = jnp.zeros((1, 1), F32)
        scale = 1.0 / (left_scale * right_scale)
        for i in range(2):
            for j in range(2):
                value = dot(xh[part(i), :], prh[:, part(j)]) + (
                    dot(xh[part(i), :], prl[:, part(j)]) + dot(xl[part(i), :], prh[:, part(j)]))
                value = value * scale
                square = square + total(value * value)
                a_buf[part(i), part(j)] = value
        count = 512.0 * 512.0
        ratio = jnp.sqrt(graft / count + 1e-12) / jnp.sqrt(square / count + 1e-12)
        for i in range(2):
            back[k, 2 * i:2 * i + 2] = (a_buf[part(i), :] * ratio).reshape(2, 4, 2, 2, 8, 512)

    def turn(k, carry):
        landed(arrive(k))
        slot(k)
        start(from_slot(k))

        @pl.when(k == 1)
        def _():
            landed(from_slot(0))
            start(in_first())

        return carry

    lax.fori_loop(0, 3, turn, 0)
    landed(from_slot(1))
    landed(from_slot(2))
    lax.fori_loop(0, cap, build_comp, 0)
    start(in_more())
    gone(out_first())
    gone(out_more())
    gone(to_first())
    gone(to_more(1))
    gone(to_more(2))
    for k in range(3):
        gone(from_slot(k))
    for copy in sum_copies:
        copy.wait_send()
    for k in range(3):
        pltpu.make_async_copy(lbuf.at[k], new_left_ref.at[0, k], io_out.at[0, k]).wait()
        pltpu.make_async_copy(rbuf.at[k], new_right_ref.at[0, k], io_out.at[1, k]).wait()
    for copies in (in_first(), in_more()):
        landed(copies)
        gone(copies)

    def take(b, carry):
        s = table_ref[OWNER, b]
        _, za, xa, _, _ = place(s)
        for h, a in enumerate((za, xa)):
            entry = jnp.minimum(table_ref[ENTRY_A + h, s], 7 + cap)
            update_ref[0, b, h * 8:h * 8 + 8] = fin[h, a, entry]
        return carry

    lax.fori_loop(0, update_ref.shape[1], take, 0)


def step(cap, ident, assign, table, gradient, left_stat, right_stat):
    vm = lambda *shape, dtype=F32: pltpu.VMEM(shape, dtype)
    half = lambda *shape: pltpu.VMEM(shape, BF16)
    dma = lambda *shape: pltpu.SemaphoreType.DMA(shape)
    any_spec = pl.BlockSpec(memory_space=pl.ANY)
    smem = pl.BlockSpec(memory_space=pltpu.SMEM)
    vmem = pl.BlockSpec(memory_space=pltpu.VMEM)
    entries = 8 + cap
    piece = (3, 4, 4, 2, 2, 8, 512)
    return pl.pallas_call(
        functools.partial(step_kernel, cap),
        out_shape=(
            jax.ShapeDtypeStruct(gradient.shape, F32),
            jax.ShapeDtypeStruct(left_stat.shape, F32),
            jax.ShapeDtypeStruct(right_stat.shape, F32),
            jax.ShapeDtypeStruct((8, 128), F32),
        ),
        in_specs=[smem, smem, vmem, any_spec, any_spec],
        out_specs=(vmem, any_spec, any_spec, vmem),
        scratch_shapes=[
            vm(2, 4, entries, 8, 512), vm(2, 4, entries, 8, 512), vm(2, 2, 8, 4, 8, 512), vm(*piece),
            vm(*piece), vm(3, 2, 8, 4, 8, 512), vm(2, 4, cap, 8, 512), vm(2, 4, entries, 8, 512),
            vm(3, 512, 512), vm(3, 512, 512), vm(4, 2, 8, 128), vm(13, 2, 8, 128),
            half(512, 512), half(512, 512), vm(512, 512), half(512, 512), half(512, 512), half(512, 512),
            half(512, 512), vm(512, 512), half(512, 512), half(512, 512), half(512, 512), half(512, 512),
            dma(4, 2, 3), dma(4, 2, 3), dma(6, 2, 7), dma(6, 2, 7), dma(10, 2), dma(13), dma(13), dma(2), dma(2, 3),
        ],
        name="step" + str(cap),
        compiler_params=pltpu.CompilerParams(collective_id=ident, has_side_effects=True, vmem_limit_bytes=58 * 2**20),
    )(assign, table, gradient, left_stat, right_stat)


def body(gradient, left_stat, right_stat, assign):
    table = pl.pallas_call(
        table_kernel,
        out_shape=jax.ShapeDtypeStruct((8, 128), jnp.int32),
        in_specs=[pl.BlockSpec(memory_space=pltpu.VMEM)],
        out_specs=pl.BlockSpec(memory_space=pltpu.VMEM),
        scratch_shapes=[pltpu.VMEM((8, 128), F32)],
        name="table",
    )(assign)
    *outs, over = step(CAP, 0, assign, table, gradient, left_stat, right_stat)

    def again(_):
        return tuple(step(FULL, 1, assign, table, gradient, left_stat, right_stat)[:3])

    return lax.cond(over[0, 0] > 0.0, again, lambda kept: kept, tuple(outs))


def solution(mesh):
    placed = P("expert", None, "shard", None)
    slots = P("expert", "shard", None, None)
    return jax.shard_map(
        body,
        mesh=mesh,
        in_specs=(placed, slots, slots, P("expert", None)),
        out_specs=(placed, slots, slots),
        check_vma=False,
    )
```

time: 94.3 us -> 88.1 us (0.934)
  Pallas kernels: 84.2 us -> 77.3 us
  other arithmetic: 1.28 us -> 0 us
  local copies, waits for them, and re-layouts: 7.99 us -> 9.19 us
    pallas_call x1 -> x2, Pallas kernels: 84.2 us -> 77.3 us  [the longest x1 76.4 us: step(): pl.pallas_call(functools.partial(step_kernel, cap), out_shape=(jax.ShapeD...]
    reduce_sum x1 -> x0, other arithmetic: 1.28 us -> none  [body(): jnp.sum(jnp.where(assign[0][None, :] == ids[:, None], slots[None, :], 0),...]
    slice x0 -> x1, local copies, waits for them, and re-layouts: none -> 1.2 us  [body(): return lax.cond(over[0, 0] > 0.0, again, lambda kept: kept, tuple(outs))]
    unnamed x5 -> x9, local copies, waits for them, and re-layouts: 7.99 us -> 8 us
where the time goes in v2:
time: 88.1 us; the launch traced here: 88 us
  Pallas kernels  77.3 us (88%)
  local copies, waits for them, and re-layouts  9.19 us (10%)
  between operations  1.32 us (1%)
    pallas_call x1, Pallas kernels, step(): pl.pallas_call(functools.partial(step_kernel, cap), out_shape=(jax.ShapeD...  76.4 us
    unnamed x9, local copies, waits for them, and re-layouts  8 us

profile of v2, /device:TPU:1, one launch (start us, length us, event | category | flops | bytes accessed | tf_op | source)
XLA Modules:
  0.0 88.0 jit_solution(7930846471359259983)
XLA Ops:
  0.6 0.9 table.1.table_ref
  1.5 0.0 copy-start
  1.5 0.0 copy-start.2
  1.5 76.4 %step8.1 = (f32[1,32,16,512]{3,2,1,0:T(8,128)}, f32[1,3,512,512]{3,2,1,0:T(8,128)}, f32[1,3,512,512]{3,2,1,0:T(8,128)}, f32[8,128]{1,0:T(8,128)}) custom-call(s32[1,96]{1,0:T(1,128)} %assign_ref.3, s32[8,128]{1,0:T(8,128)S(1)} %table.1.table_ref, f32[1,32,16,512]{3,2,1,0:T(8,128)} %grad_ref.1, f32[1,3,512,512]{3,2,1,0:T(8,128)} %left_ref.1, ...), custom_call_target="tpu_custom_call" | custom-call | tf_op jit(solution)/shard_map/step8/pallas_call | solution.py:429
  77.9 1.2 %slice.3 = f32[1,1]{1,0:T(1,128)} slice(f32[8,128]{1,0:T(8,128)} %get-tuple-element.31), slice={[0:1], [0:1]} | slice | bytes 8 | tf_op jit(solution)/shard_map/slice | solution.py:466
  79.7 0.0 copy-done
  79.8 0.0 copy-done.2
  79.8 0.2 conditional.1
  80.0 2.3 %copy.22 = f32[1,32,16,512]{3,2,1,0:T(8,128)} copy(f32[1,32,16,512]{3,2,1,0:T(8,128)} %get-tuple-element.50) | data formatting | bytes 2097152
  82.3 0.0 copy-start.1
  82.3 4.0 %copy.23 = f32[1,3,512,512]{3,2,1,0:T(8,128)} copy(f32[1,3,512,512]{3,2,1,0:T(8,128)} %get-tuple-element.51) | data formatting | bytes 6291456
  86.3 0.0 copy-done.1
  86.3 1.7 %copy.24 = f32[1,3,512,512]{3,2,1,0:T(8,128)} copy(f32[1,3,512,512]{3,2,1,0:T(8,128)S(1)} %copy-done.1) | data formatting | bytes 6291456
Async XLA Ops:
  1.5 78.3 %copy-start = (f32[1,3,512,512]{3,2,1,0:T(8,128)S(1)}, f32[1,3,512,512]{3,2,1,0:T(8,128)}, u32[]{:S(2)}) copy-start(f32[1,3,512,512]{3,2,1,0:T(8,128)} %left_ref.1) | copy-start | bytes 9437188
  1.5 78.3 %copy-start.2 = (s32[1,96]{1,0:T(1,128)S(1)}, s32[1,96]{1,0:T(1,128)}, u32[]{:S(2)}) copy-start(s32[1,96]{1,0:T(1,128)} %assign_ref.3) | copy-start | bytes 1156
  82.3 4.0 %copy-start.1 = (f32[1,3,512,512]{3,2,1,0:T(8,128)S(1)}, f32[1,3,512,512]{3,2,1,0:T(8,128)}, u32[]{:S(2)}) copy-start(f32[1,3,512,512]{3,2,1,0:T(8,128)} %get-tuple-element.52) | copy-start | bytes 9437188

commit v3 on v2

--- a/solution.py
+++ b/solution.py
@@ -47,7 +47,7 @@
     return slot - 3 * d, z, x, d & 7, z * 2 + c
 
 
-def table_kernel(assign_ref, table_ref, row):
+def fill_table(assign_ref, table_ref, row):
     shape = (128, 128)
     row[...] = jnp.full((8, 128), -1.0, F32)
     row[0:1, 0:96] = assign_ref[...].astype(F32)
@@ -70,24 +70,24 @@
         before_j = count(more_i & same & (i < j), 0)
         listed = more_i & (ga_i == (j >> 4)) & (before_i == (j & 15).astype(F32))
         spots = jnp.sum(jnp.where(listed, i.astype(F32), 0.0), axis=0, keepdims=True)
-        table_ref[LIST_A + h:LIST_A + h + 1, :] = spots.astype(jnp.int32)
+        table_ref[LIST_A + h:LIST_A + h + 1, :] = jnp.minimum(spots, 95.0).astype(jnp.int32)
         entry = jnp.where(rank_j[0:1] == 0, b_j[0:1].astype(F32), 8.0 + before_j)
-        table_ref[ENTRY_A + h:ENTRY_A + h + 1, :] = entry.astype(jnp.int32)
+        table_ref[ENTRY_A + h:ENTRY_A + h + 1, :] = jnp.clip(entry, 0.0, 23.0).astype(jnp.int32)
         over = over + count(more_j[0:1] & (before_j >= float(CAP)), 1)
     owner = jnp.sum(jnp.where(down == j.astype(F32), i.astype(F32), 0.0), axis=0, keepdims=True)
-    table_ref[OWNER:OWNER + 1, :] = owner.astype(jnp.int32)
+    table_ref[OWNER:OWNER + 1, :] = jnp.minimum(owner, 95.0).astype(jnp.int32)
     table_ref[OVER:OVER + 1, :] = jnp.broadcast_to(over, (1, 128)).astype(jnp.int32)
     table_ref[OVER + 1:8, :] = jnp.zeros((7 - OVER, 128), jnp.int32)
 
 
 def step_kernel(
     cap,
-    assign_ref, table_ref, grad_ref, left_ref, right_ref,
+    assign_ref, row_ref, gradient_ref, left_ref, right_ref,
     update_ref, new_left_ref, new_right_ref, over_ref,
     sent, mid, pad, held, back, rmid, comp, fin,
-    lbuf, rbuf, sums, sumv,
+    grad_ref, lbuf, rbuf, sums, sumv, sumy, row, table_v, table_ref,
     sh, sl, a_buf, xh, xl, yh, yl, base, plh, pll, prh, prl,
-    a_s, a_r, b_s, b_r, loc, sum_s, sum_r, io_in, io_out,
+    a_s, a_r, b_s, b_r, loc, sum_s, sum_r, y_s, y_r, io_in, io_out,
 ):
     e = lax.axis_index("expert")
     me = lax.axis_index("shard")
@@ -106,19 +106,20 @@
     barrier = pltpu.get_barrier_semaphore()
     for d in range(1, 4):
         pl.semaphore_signal(barrier, inc=1, device_id=(lax.rem(e + d, 4), me), device_id_type=MESH)
-    for d in range(1, 8):
-        pl.semaphore_signal(barrier, inc=1, device_id=device(0, z, lax.rem(spot[0] + d, 8)), device_id_type=MESH)
-    for d in range(1, 4):
-        for f in range(2):
-            pl.semaphore_signal(
-                barrier, inc=1, device_id=(e, lax.rem(z + d, 4) * 8 + x * 2 + lax.rem(c + f, 2)), device_id_type=MESH)
-
+    for d in range(1, 32):
+        pl.semaphore_signal(barrier, inc=1, device_id=(e, lax.rem(me + d, 32)), device_id_type=MESH)
+
+    fetch = pltpu.make_async_copy(gradient_ref, grad_ref, io_in.at[2])
+    fetch.start()
     loads = [
         pltpu.make_async_copy(left_ref.at[0], lbuf, io_in.at[0]),
         pltpu.make_async_copy(right_ref.at[0], rbuf, io_in.at[1]),
     ]
     for copy in loads:
         copy.start()
+    fill_table(row_ref, table_v, row)
+    lists = pltpu.make_async_copy(table_v, table_ref, io_in.at[3])
+    lists.start()
 
     def square_sum(b, acc):
         rows = grad_ref[0, b]
@@ -127,11 +128,15 @@
             acc = acc + sq[0:8, q * 128:(q + 1) * 128] + sq[8:16, q * 128:(q + 1) * 128]
         return acc
 
-    sums[0, 0] = lax.fori_loop(0, grad_ref.shape[1], square_sum, jnp.zeros((8, 128), F32))
-    sums[0, 1] = jnp.full((8, 128), table_ref[OVER, 0].astype(F32), F32)
+    fetch.wait()
+    squares = lax.fori_loop(0, grad_ref.shape[1], square_sum, jnp.zeros((8, 128), F32))
+    sums[...] = jnp.sum(squares, axis=0, keepdims=True)
+
+    def look(line, at, top):
+        return jnp.clip(table_ref[line, at], 0, top)
 
     def build_first(d, carry):
-        block = jnp.maximum(assign_ref[0, d * 3], 0)
+        block = jnp.clip(assign_ref[0, d * 3], 0, 31)
         rows = grad_ref[0, block]
         zd, xd, cd = lax.div(d, 8), lax.rem(lax.div(d, 2), 4), lax.rem(d, 2)
         sent[0, zd, xd * 2 + cd] = rows[0:8]
@@ -141,14 +146,14 @@
     def build_more(n, carry):
         a, j = lax.div(n, cap), lax.rem(n, cap)
         for h in range(2):
-            block = jnp.maximum(assign_ref[0, table_ref[LIST_A + h, a * 16 + j]], 0)
+            block = jnp.clip(assign_ref[0, look(LIST_A + h, a * 16 + j, 95)], 0, 31)
             sent[h, a, 8 + j] = grad_ref[0, block, h * 8:h * 8 + 8]
         return carry
 
     def build_pad(k):
         def one(b, carry):
             for h in range(2):
-                entry = jnp.minimum(table_ref[ENTRY_A + h, index(h, group[h], b) * 3 + k], 7 + cap)
+                entry = look(ENTRY_A + h, index(h, group[h], b) * 3 + k, 7 + cap)
                 pad[k - 1, h, b] = mid[h, :, entry]
             return carry
 
@@ -156,7 +161,7 @@
 
     def build_comp(j, carry):
         for h in range(2):
-            rank, _, _, b0, b1 = place(table_ref[LIST_A + h, group[h] * 16 + j])
+            rank, _, _, b0, b1 = place(look(LIST_A + h, group[h] * 16 + j, 95))
             comp[h, :, j] = rmid[rank, h, (b0, b1)[h]]
         return carry
 
@@ -221,43 +226,42 @@
             copy.wait_send()
 
     lax.fori_loop(0, 32, build_first, 0)
-    pl.semaphore_wait(barrier, 16)
+    lists.wait()
+    lax.fori_loop(0, 4 * cap, build_more, 0)
+    pl.semaphore_wait(barrier, 34)
 
     sum_copies = []
-
-    def sum_stage(stage, at, peers):
-        copies = []
-        for i, peer in enumerate(peers):
-            copies.append(pltpu.make_async_remote_copy(
-                src_ref=sums.at[stage], dst_ref=sumv.at[at + i],
-                send_sem=sum_s.at[at + i], recv_sem=sum_r.at[at + i],
-                device_id=peer, device_id_type=MESH))
-        for copy in copies:
-            copy.start()
-        sum_copies.extend(copies)
-        return copies
-
-    def sum_take(stage, at, copies):
-        acc = sums[stage]
-        for i, copy in enumerate(copies):
-            copy.wait_recv()
-            acc = acc + sumv[at + i]
-        sums[stage + 1] = acc
-
-    s0 = sum_stage(0, 0, [(lax.rem(e + d, 4), me) for d in range(1, 4)])
+    for d in range(1, 32):
+        sum_copies.append(pltpu.make_async_remote_copy(
+            src_ref=sums, dst_ref=sumv.at[d - 1], send_sem=sum_s.at[d - 1], recv_sem=sum_r.at[d - 1],
+            device_id=(e, lax.rem(me + d, 32)), device_id_type=MESH))
+    for copy in sum_copies:
+        copy.start()
     start(out_first())
-    lax.fori_loop(0, 4 * cap, build_more, 0)
     start(out_more())
-    sum_take(0, 0, s0)
-    s1 = sum_stage(1, 3, [device(0, lax.rem(z + d, 4), spot[0]) for d in range(1, 4)])
-    sum_take(1, 3, s1)
-    s2 = sum_stage(2, 6, [device(0, z, lax.rem(spot[0] + d, 8)) for d in range(1, 8)])
+    acc = sums[...]
+    for d, copy in enumerate(sum_copies):
+        copy.wait_recv()
+        acc = acc + sumv[d]
+    sumy[0, 0:1, :] = acc
+    sumy[0, 1:2, :] = jnp.full((1, 128), table_ref[OVER, 0].astype(F32), F32)
+    sumy[0, 2:8, :] = jnp.zeros((6, 128), F32)
+    y_copies = []
+    for d in range(1, 4):
+        y_copies.append(pltpu.make_async_remote_copy(
+            src_ref=sumy.at[0], dst_ref=sumy.at[d], send_sem=y_s.at[d - 1], recv_sem=y_r.at[d - 1],
+            device_id=(lax.rem(e + d, 4), me), device_id_type=MESH))
+    for copy in y_copies:
+        copy.start()
     landed(out_first())
     start(to_first())
-    sum_take(2, 6, s2)
-    mean_square = total(sums[3, 0]) / (4.0 * 32.0 * 512.0 * 512.0)
+    acc = sumy[0]
+    for d, copy in enumerate(y_copies):
+        copy.wait_recv()
+        acc = acc + sumy[d + 1]
+    mean_square = total(acc[0:1, :]) / (4.0 * 32.0 * 512.0 * 512.0)
     factor = jnp.minimum(1.0, 1.0 / jnp.sqrt(mean_square + 1e-06))
-    over_ref[...] = sums[3, 1]
+    over_ref[...] = acc
     landed(out_more())
     build_pad(1)
     start(to_more(1))
@@ -397,7 +401,7 @@
     gone(to_more(2))
     for k in range(3):
         gone(from_slot(k))
-    for copy in sum_copies:
+    for copy in sum_copies + y_copies:
         copy.wait_send()
     for k in range(3):
         pltpu.make_async_copy(lbuf.at[k], new_left_ref.at[0, k], io_out.at[0, k]).wait()
@@ -407,17 +411,17 @@
         gone(copies)
 
     def take(b, carry):
-        s = table_ref[OWNER, b]
+        s = look(OWNER, b, 95)
         _, za, xa, _, _ = place(s)
         for h, a in enumerate((za, xa)):
-            entry = jnp.minimum(table_ref[ENTRY_A + h, s], 7 + cap)
+            entry = look(ENTRY_A + h, s, 7 + cap)
             update_ref[0, b, h * 8:h * 8 + 8] = fin[h, a, entry]
         return carry
 
     lax.fori_loop(0, update_ref.shape[1], take, 0)
 
 
-def step(cap, ident, assign, table, gradient, left_stat, right_stat):
+def step(cap, ident, assign, gradient, left_stat, right_stat):
     vm = lambda *shape, dtype=F32: pltpu.VMEM(shape, dtype)
     half = lambda *shape: pltpu.VMEM(shape, BF16)
     dma = lambda *shape: pltpu.SemaphoreType.DMA(shape)
@@ -434,36 +438,30 @@
             jax.ShapeDtypeStruct(right_stat.shape, F32),
             jax.ShapeDtypeStruct((8, 128), F32),
         ),
-        in_specs=[smem, smem, vmem, any_spec, any_spec],
+        in_specs=[smem, vmem, any_spec, any_spec, any_spec],
         out_specs=(vmem, any_spec, any_spec, vmem),
         scratch_shapes=[
             vm(2, 4, entries, 8, 512), vm(2, 4, entries, 8, 512), vm(2, 2, 8, 4, 8, 512), vm(*piece),
             vm(*piece), vm(3, 2, 8, 4, 8, 512), vm(2, 4, cap, 8, 512), vm(2, 4, entries, 8, 512),
-            vm(3, 512, 512), vm(3, 512, 512), vm(4, 2, 8, 128), vm(13, 2, 8, 128),
+            vm(1, 32, 16, 512), vm(3, 512, 512), vm(3, 512, 512), vm(1, 128), vm(31, 1, 128), vm(4, 8, 128),
+            vm(8, 128), vm(8, 128, dtype=jnp.int32), pltpu.SMEM((8, 128), jnp.int32),
             half(512, 512), half(512, 512), vm(512, 512), half(512, 512), half(512, 512), half(512, 512),
             half(512, 512), vm(512, 512), half(512, 512), half(512, 512), half(512, 512), half(512, 512),
-            dma(4, 2, 3), dma(4, 2, 3), dma(6, 2, 7), dma(6, 2, 7), dma(10, 2), dma(13), dma(13), dma(2), dma(2, 3),
+            dma(4, 2, 3), dma(4, 2, 3), dma(6, 2, 7), dma(6, 2, 7), dma(10, 2), dma(31), dma(31), dma(3), dma(3),
+            dma(4), dma(2, 3),
         ],
         name="step" + str(cap),
         compiler_params=pltpu.CompilerParams(collective_id=ident, has_side_effects=True, vmem_limit_bytes=58 * 2**20),
-    )(assign, table, gradient, left_stat, right_stat)
+    )(assign, assign, gradient, left_stat, right_stat)
 
 
 def body(gradient, left_stat, right_stat, assign):
-    table = pl.pallas_call(
-        table_kernel,
-        out_shape=jax.ShapeDtypeStruct((8, 128), jnp.int32),
-        in_specs=[pl.BlockSpec(memory_space=pltpu.VMEM)],
-        out_specs=pl.BlockSpec(memory_space=pltpu.VMEM),
-        scratch_shapes=[pltpu.VMEM((8, 128), F32)],
-        name="table",
-    )(assign)
-    *outs, over = step(CAP, 0, assign, table, gradient, left_stat, right_stat)
+    *outs, over = step(CAP, 0, assign, gradient, left_stat, right_stat)
 
     def again(_):
-        return tuple(step(FULL, 1, assign, table, gradient, left_stat, right_stat)[:3])
-
-    return lax.cond(over[0, 0] > 0.0, again, lambda kept: kept, tuple(outs))
+        return tuple(step(FULL, 1, assign, gradient, left_stat, right_stat)[:3])
+
+    return lax.cond(over[1, 0] > 0.0, again, lambda kept: kept, tuple(outs))
 
 
 def solution(mesh):

time: 88.1 us -> 84.6 us (0.960)
  Pallas kernels: 77.3 us -> 73.4 us
    pallas_call x1, Pallas kernels: 76.4 us -> 73.4 us  [step(): pl.pallas_call(functools.partial(step_kernel, cap), out_shape=(jax.ShapeD...]
where the time goes in v3:
time: 84.6 us; the launch traced here: 84.1 us
  Pallas kernels  73.4 us (87%)
  local copies, waits for them, and re-layouts  9.2 us (11%)
  between operations  1.33 us (2%)
    pallas_call x1, Pallas kernels, step(): pl.pallas_call(functools.partial(step_kernel, cap), out_shape=(jax.ShapeD...  73.4 us
    unnamed x9, local copies, waits for them, and re-layouts  8 us

profile of v3, /device:TPU:1, one launch (start us, length us, event | category | flops | bytes accessed | tf_op | source)
XLA Modules:
  0.0 84.1 jit_solution(16076138680544238090)
XLA Ops:
  0.6 0.0 copy-start
  0.6 0.0 copy-start.2
  0.7 73.4 %step8.1 = (f32[1,32,16,512]{3,2,1,0:T(8,128)}, f32[1,3,512,512]{3,2,1,0:T(8,128)}, f32[1,3,512,512]{3,2,1,0:T(8,128)}, f32[8,128]{1,0:T(8,128)}) custom-call(s32[1,96]{1,0:T(1,128)} %row_ref.1, s32[1,96]{1,0:T(1,128)} %row_ref.1, f32[1,32,16,512]{3,2,1,0:T(8,128)} %gradient_ref.1, f32[1,3,512,512]{3,2,1,0:T(8,128)} %left_ref.1, f32[1,3,512,512]{3,2,1,0:T(8,128)} %right_ref.1), custom_call_target="tpu_custom_call" | custom-call | tf_op jit(solution)/shard_map/step8/pallas_call | solution.py:433
  74.0 1.2 %slice.3 = f32[1,1]{1,0:T(1,128)} slice(f32[8,128]{1,0:T(8,128)} %get-tuple-element.28), slice={[1:2], [0:1]} | slice | bytes 8 | tf_op jit(solution)/shard_map/slice | solution.py:464
  75.9 0.0 copy-done
  75.9 0.0 copy-done.2
  75.9 0.2 conditional.1
  76.1 2.3 %copy.22 = f32[1,32,16,512]{3,2,1,0:T(8,128)} copy(f32[1,32,16,512]{3,2,1,0:T(8,128)} %get-tuple-element.47) | data formatting | bytes 2097152
  78.4 0.0 copy-start.1
  78.4 4.0 %copy.23 = f32[1,3,512,512]{3,2,1,0:T(8,128)} copy(f32[1,3,512,512]{3,2,1,0:T(8,128)} %get-tuple-element.48) | data formatting | bytes 6291456
  82.4 0.0 copy-done.1
  82.4 1.7 %copy.24 = f32[1,3,512,512]{3,2,1,0:T(8,128)} copy(f32[1,3,512,512]{3,2,1,0:T(8,128)S(1)} %copy-done.1) | data formatting | bytes 6291456
Async XLA Ops:
  0.6 75.2 %copy-start = (f32[1,3,512,512]{3,2,1,0:T(8,128)S(1)}, f32[1,3,512,512]{3,2,1,0:T(8,128)}, u32[]{:S(2)}) copy-start(f32[1,3,512,512]{3,2,1,0:T(8,128)} %left_ref.1) | copy-start | bytes 9437188
  0.6 75.2 %copy-start.2 = (s32[1,96]{1,0:T(1,128)S(1)}, s32[1,96]{1,0:T(1,128)}, u32[]{:S(2)}) copy-start(s32[1,96]{1,0:T(1,128)} %row_ref.1) | copy-start | bytes 1156
  78.4 4.0 %copy-start.1 = (f32[1,3,512,512]{3,2,1,0:T(8,128)S(1)}, f32[1,3,512,512]{3,2,1,0:T(8,128)}, u32[]{:S(2)}) copy-start(f32[1,3,512,512]{3,2,1,0:T(8,128)} %get-tuple-element.49) | copy-start | bytes 9437188

commit v4 on v3

--- a/solution.py
+++ b/solution.py
@@ -85,13 +85,14 @@
     assign_ref, row_ref, gradient_ref, left_ref, right_ref,
     update_ref, new_left_ref, new_right_ref, over_ref,
     sent, mid, pad, held, back, rmid, comp, fin,
-    grad_ref, lbuf, rbuf, sums, sumv, sumy, row, table_v, table_ref,
+    grad_ref, sums, sumv, sumy, row, table_v, table_ref,
     sh, sl, a_buf, xh, xl, yh, yl, base, plh, pll, prh, prl,
-    a_s, a_r, b_s, b_r, loc, sum_s, sum_r, y_s, y_r, io_in, io_out,
+    a_s, a_r, b_s, b_r, loc, sum_s, sum_r, y_s, y_r, io_in,
 ):
     e = lax.axis_index("expert")
     me = lax.axis_index("shard")
     z, x, c = lax.div(me, 8), lax.rem(lax.div(me, 2), 4), lax.rem(me, 2)
+    lbuf, rbuf = new_left_ref.at[0], new_right_ref.at[0]
     group = (z, x)
     spot = (x * 2 + c, z * 2 + c)
 
@@ -111,16 +112,6 @@
 
     fetch = pltpu.make_async_copy(gradient_ref, grad_ref, io_in.at[2])
     fetch.start()
-    loads = [
-        pltpu.make_async_copy(left_ref.at[0], lbuf, io_in.at[0]),
-        pltpu.make_async_copy(right_ref.at[0], rbuf, io_in.at[1]),
-    ]
-    for copy in loads:
-        copy.start()
-    fill_table(row_ref, table_v, row)
-    lists = pltpu.make_async_copy(table_v, table_ref, io_in.at[3])
-    lists.start()
-
     def square_sum(b, acc):
         rows = grad_ref[0, b]
         sq = rows * rows
@@ -128,9 +119,6 @@
             acc = acc + sq[0:8, q * 128:(q + 1) * 128] + sq[8:16, q * 128:(q + 1) * 128]
         return acc
 
-    fetch.wait()
-    squares = lax.fori_loop(0, grad_ref.shape[1], square_sum, jnp.zeros((8, 128), F32))
-    sums[...] = jnp.sum(squares, axis=0, keepdims=True)
 
     def look(line, at, top):
         return jnp.clip(table_ref[line, at], 0, top)
@@ -157,7 +145,7 @@
                 pad[k - 1, h, b] = mid[h, :, entry]
             return carry
 
-        lax.fori_loop(0, 8, one, 0)
+        lax.fori_loop(0, 8, one, 0, unroll=4)
 
     def build_comp(j, carry):
         for h in range(2):
@@ -225,10 +213,13 @@
         for copy in copies[0]:
             copy.wait_send()
 
-    lax.fori_loop(0, 32, build_first, 0)
-    lists.wait()
-    lax.fori_loop(0, 4 * cap, build_more, 0)
+    fetch.wait()
+    lax.fori_loop(0, 32, build_first, 0, unroll=8)
     pl.semaphore_wait(barrier, 34)
+    start(out_first())
+
+    squares = lax.fori_loop(0, grad_ref.shape[1], square_sum, jnp.zeros((8, 128), F32), unroll=8)
+    sums[...] = jnp.sum(squares, axis=0, keepdims=True)
 
     sum_copies = []
     for d in range(1, 32):
@@ -237,8 +228,18 @@
             device_id=(e, lax.rem(me + d, 32)), device_id_type=MESH))
     for copy in sum_copies:
         copy.start()
-    start(out_first())
+    fill_table(row_ref, table_v, row)
+    lists = pltpu.make_async_copy(table_v, table_ref, io_in.at[3])
+    lists.start()
+    lists.wait()
+    lax.fori_loop(0, 4 * cap, build_more, 0, unroll=4)
     start(out_more())
+    loads = [
+        pltpu.make_async_copy(left_ref.at[0], lbuf, io_in.at[0]),
+        pltpu.make_async_copy(right_ref.at[0], rbuf, io_in.at[1]),
+    ]
+    for copy in loads:
+        copy.start()
     acc = sums[...]
     for d, copy in enumerate(sum_copies):
         copy.wait_recv()
@@ -352,12 +353,10 @@
             lbuf, k, live,
             lambda i, j: dot(sh[part(i), :], sh[part(j), :], nt),
             lambda i, j: dot(sh[part(i), :], sl[part(j), :], nt)), plh, pll)
-        pltpu.make_async_copy(lbuf.at[k], new_left_ref.at[0, k], io_out.at[0, k]).start()
         right_scale = root(stat(
             rbuf, k, live,
             lambda i, j: dot(sh[:, part(i)], sh[:, part(j)], tn),
             lambda i, j: dot(sh[:, part(i)], sl[:, part(j)], tn)), prh, prl)
-        pltpu.make_async_copy(rbuf.at[k], new_right_ref.at[0, k], io_out.at[1, k]).start()
 
         for i in range(2):
             for j in range(2):
@@ -381,18 +380,14 @@
         landed(arrive(k))
         slot(k)
         start(from_slot(k))
-
-        @pl.when(k == 1)
-        def _():
-            landed(from_slot(0))
-            start(in_first())
-
         return carry
 
     lax.fori_loop(0, 3, turn, 0)
+    landed(from_slot(0))
+    start(in_first())
     landed(from_slot(1))
     landed(from_slot(2))
-    lax.fori_loop(0, cap, build_comp, 0)
+    lax.fori_loop(0, cap, build_comp, 0, unroll=4)
     start(in_more())
     gone(out_first())
     gone(out_more())
@@ -403,9 +398,6 @@
         gone(from_slot(k))
     for copy in sum_copies + y_copies:
         copy.wait_send()
-    for k in range(3):
-        pltpu.make_async_copy(lbuf.at[k], new_left_ref.at[0, k], io_out.at[0, k]).wait()
-        pltpu.make_async_copy(rbuf.at[k], new_right_ref.at[0, k], io_out.at[1, k]).wait()
     for copies in (in_first(), in_more()):
         landed(copies)
         gone(copies)
@@ -418,7 +410,7 @@
             update_ref[0, b, h * 8:h * 8 + 8] = fin[h, a, entry]
         return carry
 
-    lax.fori_loop(0, update_ref.shape[1], take, 0)
+    lax.fori_loop(0, update_ref.shape[1], take, 0, unroll=4)
 
 
 def step(cap, ident, assign, gradient, left_stat, right_stat):
@@ -439,29 +431,52 @@
             jax.ShapeDtypeStruct((8, 128), F32),
         ),
         in_specs=[smem, vmem, any_spec, any_spec, any_spec],
-        out_specs=(vmem, any_spec, any_spec, vmem),
+        out_specs=(vmem, vmem, vmem, vmem),
         scratch_shapes=[
             vm(2, 4, entries, 8, 512), vm(2, 4, entries, 8, 512), vm(2, 2, 8, 4, 8, 512), vm(*piece),
             vm(*piece), vm(3, 2, 8, 4, 8, 512), vm(2, 4, cap, 8, 512), vm(2, 4, entries, 8, 512),
-            vm(1, 32, 16, 512), vm(3, 512, 512), vm(3, 512, 512), vm(1, 128), vm(31, 1, 128), vm(4, 8, 128),
+            vm(1, 32, 16, 512), vm(1, 128), vm(31, 1, 128), vm(4, 8, 128),
             vm(8, 128), vm(8, 128, dtype=jnp.int32), pltpu.SMEM((8, 128), jnp.int32),
             half(512, 512), half(512, 512), vm(512, 512), half(512, 512), half(512, 512), half(512, 512),
             half(512, 512), vm(512, 512), half(512, 512), half(512, 512), half(512, 512), half(512, 512),
             dma(4, 2, 3), dma(4, 2, 3), dma(6, 2, 7), dma(6, 2, 7), dma(10, 2), dma(31), dma(31), dma(3), dma(3),
-            dma(4), dma(2, 3),
+            dma(4),
         ],
         name="step" + str(cap),
-        compiler_params=pltpu.CompilerParams(collective_id=ident, has_side_effects=True, vmem_limit_bytes=58 * 2**20),
+        compiler_params=pltpu.CompilerParams(collective_id=ident, has_side_effects=True, vmem_limit_bytes=(44 if cap == CAP else 63) * 2**20),
     )(assign, assign, gradient, left_stat, right_stat)
+
+
+def store_kernel(update_in, left_in, right_in, update_out, left_out, right_out):
+    left_out[...] = left_in[...]
+    right_out[...] = right_in[...]
+
+    @pl.when(pl.program_id(0) == 0)
+    def _():
+        update_out[...] = update_in[...]
+
+
+def store(outs):
+    slot_spec = pl.BlockSpec((1, 1, 512, 512), lambda k: (0, k, 0, 0))
+    whole = pl.BlockSpec((1, 32, 16, 512), lambda k: (0, 0, 0, 0))
+    return pl.pallas_call(
+        store_kernel,
+        grid=(3,),
+        out_shape=tuple(jax.ShapeDtypeStruct(out.shape, out.dtype) for out in outs),
+        in_specs=[whole, slot_spec, slot_spec],
+        out_specs=(whole, slot_spec, slot_spec),
+        name="store",
+        compiler_params=pltpu.CompilerParams(vmem_limit_bytes=30 * 2**20),
+    )(*outs)
 
 
 def body(gradient, left_stat, right_stat, assign):
     *outs, over = step(CAP, 0, assign, gradient, left_stat, right_stat)
 
     def again(_):
-        return tuple(step(FULL, 1, assign, gradient, left_stat, right_stat)[:3])
-
-    return lax.cond(over[1, 0] > 0.0, again, lambda kept: kept, tuple(outs))
+        return store(step(FULL, 1, assign, gradient, left_stat, right_stat)[:3])
+
+    return lax.cond(over[1, 0] > 0.0, again, lambda kept: kept, store(outs))
 
 
 def solution(mesh):

time: 84.6 us -> 76.7 us (0.907)
  local copies, waits for them, and re-layouts: 9.2 us -> 0.52 us
    unnamed x9 -> x2, local copies, waits for them, and re-layouts: 8 us -> 0.01 us
    pallas_call x0 -> x1, Pallas kernels: none -> 3.29 us  [store(): pl.pallas_call(store_kernel, grid=(3,), out_shape=tuple((jax.ShapeDtypeSt...]
    pallas_call x1, Pallas kernels: 73.4 us -> 70.6 us  [step(): pl.pallas_call(functools.partial(step_kernel, cap), out_shape=(jax.ShapeD...]
where the time goes in v4:
time: 76.7 us; the launch traced here: 75.7 us
  Pallas kernels  73.9 us (96%)
  between operations  1.31 us (2%)
    pallas_call x1, Pallas kernels, step(): pl.pallas_call(functools.partial(step_kernel, cap), out_shape=(jax.ShapeD...  70.6 us
    pallas_call x1, Pallas kernels, store(): pl.pallas_call(store_kernel, grid=(3,), out_shape=tuple((jax.ShapeDtypeSt...  3.29 us

profile of v4, /device:TPU:1, one launch (start us, length us, event | category | flops | bytes accessed | tf_op | source)
XLA Modules:
  0.0 75.7 jit_solution(4908082372108380492)
XLA Ops:
  0.6 0.0 copy-start.3
  0.6 70.6 %step8.1 = (f32[1,32,16,512]{3,2,1,0:T(8,128)S(1)}, f32[1,3,512,512]{3,2,1,0:T(8,128)S(1)}, f32[1,3,512,512]{3,2,1,0:T(8,128)S(1)}, f32[8,128]{1,0:T(8,128)S(1)}) custom-call(s32[1,96]{1,0:T(1,128)} %row_ref.1, s32[1,96]{1,0:T(1,128)} %row_ref.1, f32[1,32,16,512]{3,2,1,0:T(8,128)} %gradient_ref.1, f32[1,3,512,512]{3,2,1,0:T(8,128)} %left_ref.1, ...), custom_call_target="tpu_custom_call" | custom-call | tf_op jit(solution)/shard_map/step8/pallas_call | solution.py:425
  71.3 0.5 slice.3
  72.4 0.0 copy-done.3
  72.4 3.3 %store.3 = (f32[1,32,16,512]{3,2,1,0:T(8,128)}, f32[1,3,512,512]{3,2,1,0:T(8,128)}, f32[1,3,512,512]{3,2,1,0:T(8,128)}) custom-call(f32[1,32,16,512]{3,2,1,0:T(8,128)S(1)} %get-tuple-element.29.update_in, f32[1,3,512,512]{3,2,1,0:T(8,128)S(1)} %get-tuple-element.30.left_in, f32[1,3,512,512]{3,2,1,0:T(8,128)S(1)} %get-tuple-element.31.right_in), custom_call_target="tpu_custom_call" | custom-call | tf_op jit(solution)/shard_map/store/pallas_call | solution.py:462
  (1 shorter events, 0.0 us)
Async XLA Ops:
  0.6 71.8 %copy-start.3 = (s32[1,96]{1,0:T(1,128)S(1)}, s32[1,96]{1,0:T(1,128)}, u32[]{:S(2)}) copy-start(s32[1,96]{1,0:T(1,128)} %row_ref.1) | copy-start | bytes 1156

commit v5 on v4

--- a/solution.py
+++ b/solution.py
@@ -82,12 +82,12 @@
 
 def step_kernel(
     cap,
-    assign_ref, row_ref, gradient_ref, left_ref, right_ref,
+    slots_ref, gradient_ref, left_ref, right_ref,
     update_ref, new_left_ref, new_right_ref, over_ref,
     sent, mid, pad, held, back, rmid, comp, fin,
-    grad_ref, sums, sumv, sumy, row, table_v, table_ref,
+    assign_ref, row_ref, grad_ref, sums, sumv, row, table_v, table_ref,
     sh, sl, a_buf, xh, xl, yh, yl, base, plh, pll, prh, prl,
-    a_s, a_r, b_s, b_r, loc, sum_s, sum_r, y_s, y_r, io_in,
+    a_s, a_r, b_s, b_r, loc, sum_s, sum_r, io_in,
 ):
     e = lax.axis_index("expert")
     me = lax.axis_index("shard")
@@ -104,14 +104,23 @@
     def index(h, a, b):
         return device(h, a, b)[1]
 
+    fetches = [
+        pltpu.make_async_copy(slots_ref, assign_ref, io_in.at[4]),
+        pltpu.make_async_copy(gradient_ref, grad_ref, io_in.at[2]),
+        pltpu.make_async_copy(slots_ref, row_ref, io_in.at[5]),
+    ]
+    for copy in fetches:
+        copy.start()
     barrier = pltpu.get_barrier_semaphore()
+    for d in range(1, 8):
+        pl.semaphore_signal(barrier, inc=1, device_id=device(0, z, lax.rem(spot[0] + d, 8)), device_id_type=MESH)
+    for d in range(1, 4):
+        for f in range(2):
+            pl.semaphore_signal(
+                barrier, inc=1, device_id=(e, lax.rem(z + d, 4) * 8 + x * 2 + lax.rem(c + f, 2)), device_id_type=MESH)
     for d in range(1, 4):
         pl.semaphore_signal(barrier, inc=1, device_id=(lax.rem(e + d, 4), me), device_id_type=MESH)
-    for d in range(1, 32):
-        pl.semaphore_signal(barrier, inc=1, device_id=(e, lax.rem(me + d, 32)), device_id_type=MESH)
-
-    fetch = pltpu.make_async_copy(gradient_ref, grad_ref, io_in.at[2])
-    fetch.start()
+
     def square_sum(b, acc):
         rows = grad_ref[0, b]
         sq = rows * rows
@@ -213,26 +222,45 @@
         for copy in copies[0]:
             copy.wait_send()
 
-    fetch.wait()
+    for copy in fetches:
+        copy.wait()
     lax.fori_loop(0, 32, build_first, 0, unroll=8)
-    pl.semaphore_wait(barrier, 34)
+    pl.semaphore_wait(barrier, 16)
     start(out_first())
 
-    squares = lax.fori_loop(0, grad_ref.shape[1], square_sum, jnp.zeros((8, 128), F32), unroll=8)
-    sums[...] = jnp.sum(squares, axis=0, keepdims=True)
-
-    sum_copies = []
-    for d in range(1, 32):
-        sum_copies.append(pltpu.make_async_remote_copy(
-            src_ref=sums, dst_ref=sumv.at[d - 1], send_sem=sum_s.at[d - 1], recv_sem=sum_r.at[d - 1],
-            device_id=(e, lax.rem(me + d, 32)), device_id_type=MESH))
-    for copy in sum_copies:
-        copy.start()
     fill_table(row_ref, table_v, row)
     lists = pltpu.make_async_copy(table_v, table_ref, io_in.at[3])
     lists.start()
+    squares = lax.fori_loop(0, grad_ref.shape[1], square_sum, jnp.zeros((8, 128), F32), unroll=8)
+    sums[0, 0:1, :] = jnp.sum(squares, axis=0, keepdims=True)
+    sums[0, 1:2, :] = table_v[OVER:OVER + 1, :].astype(F32)
+    sums[0, 2:8, :] = jnp.zeros((6, 128), F32)
+    sum_copies = []
+
+    def sum_send(stage, at, peers):
+        copies = []
+        for i, peer in enumerate(peers):
+            copies.append(pltpu.make_async_remote_copy(
+                src_ref=sums.at[stage], dst_ref=sumv.at[at + i],
+                send_sem=sum_s.at[at + i], recv_sem=sum_r.at[at + i],
+                device_id=peer, device_id_type=MESH))
+        for copy in copies:
+            copy.start()
+        sum_copies.extend(copies)
+        return copies
+
+    def sum_take(stage, at, copies):
+        acc = sums[stage]
+        for i, copy in enumerate(copies):
+            copy.wait_recv()
+            acc = acc + sumv[at + i]
+        sums[stage + 1] = acc
+
+    s0 = sum_send(0, 0, [(lax.rem(e + d, 4), me) for d in range(1, 4)])
     lists.wait()
     lax.fori_loop(0, 4 * cap, build_more, 0, unroll=4)
+    sum_take(0, 0, s0)
+    s1 = sum_send(1, 3, [device(0, lax.rem(z + d, 4), spot[0]) for d in range(1, 4)])
     start(out_more())
     loads = [
         pltpu.make_async_copy(left_ref.at[0], lbuf, io_in.at[0]),
@@ -240,34 +268,19 @@
     ]
     for copy in loads:
         copy.start()
-    acc = sums[...]
-    for d, copy in enumerate(sum_copies):
-        copy.wait_recv()
-        acc = acc + sumv[d]
-    sumy[0, 0:1, :] = acc
-    sumy[0, 1:2, :] = jnp.full((1, 128), table_ref[OVER, 0].astype(F32), F32)
-    sumy[0, 2:8, :] = jnp.zeros((6, 128), F32)
-    y_copies = []
-    for d in range(1, 4):
-        y_copies.append(pltpu.make_async_remote_copy(
-            src_ref=sumy.at[0], dst_ref=sumy.at[d], send_sem=y_s.at[d - 1], recv_sem=y_r.at[d - 1],
-            device_id=(lax.rem(e + d, 4), me), device_id_type=MESH))
-    for copy in y_copies:
-        copy.start()
     landed(out_first())
+    sum_take(1, 3, s1)
+    s2 = sum_send(2, 6, [device(0, z, lax.rem(spot[0] + d, 8)) for d in range(1, 8)])
     start(to_first())
-    acc = sumy[0]
-    for d, copy in enumerate(y_copies):
-        copy.wait_recv()
-        acc = acc + sumy[d + 1]
-    mean_square = total(acc[0:1, :]) / (4.0 * 32.0 * 512.0 * 512.0)
-    factor = jnp.minimum(1.0, 1.0 / jnp.sqrt(mean_square + 1e-06))
-    over_ref[...] = acc
     landed(out_more())
     build_pad(1)
     start(to_more(1))
     build_pad(2)
     start(to_more(2))
+    sum_take(2, 6, s2)
+    mean_square = total(sums[3, 0:1, :]) / (4.0 * 32.0 * 512.0 * 512.0)
+    factor = jnp.minimum(1.0, 1.0 / jnp.sqrt(mean_square + 1e-06))
+    over_ref[...] = sums[3]
     for copy in loads:
         copy.wait()
 
@@ -396,7 +409,7 @@
     gone(to_more(2))
     for k in range(3):
         gone(from_slot(k))
-    for copy in sum_copies + y_copies:
+    for copy in sum_copies:
         copy.wait_send()
     for copies in (in_first(), in_more()):
         landed(copies)
@@ -418,7 +431,6 @@
     half = lambda *shape: pltpu.VMEM(shape, BF16)
     dma = lambda *shape: pltpu.SemaphoreType.DMA(shape)
     any_spec = pl.BlockSpec(memory_space=pl.ANY)
-    smem = pl.BlockSpec(memory_space=pltpu.SMEM)
     vmem = pl.BlockSpec(memory_space=pltpu.VMEM)
     entries = 8 + cap
     piece = (3, 4, 4, 2, 2, 8, 512)
@@ -430,21 +442,21 @@
             jax.ShapeDtypeStruct(right_stat.shape, F32),
             jax.ShapeDtypeStruct((8, 128), F32),
         ),
-        in_specs=[smem, vmem, any_spec, any_spec, any_spec],
+        in_specs=[any_spec] * 4,
         out_specs=(vmem, vmem, vmem, vmem),
         scratch_shapes=[
             vm(2, 4, entries, 8, 512), vm(2, 4, entries, 8, 512), vm(2, 2, 8, 4, 8, 512), vm(*piece),
             vm(*piece), vm(3, 2, 8, 4, 8, 512), vm(2, 4, cap, 8, 512), vm(2, 4, entries, 8, 512),
-            vm(1, 32, 16, 512), vm(1, 128), vm(31, 1, 128), vm(4, 8, 128),
+            pltpu.SMEM((1, 96), jnp.int32), vm(1, 96, dtype=jnp.int32), vm(1, 32, 16, 512), vm(4, 8, 128), vm(13, 8, 128),
             vm(8, 128), vm(8, 128, dtype=jnp.int32), pltpu.SMEM((8, 128), jnp.int32),
             half(512, 512), half(512, 512), vm(512, 512), half(512, 512), half(512, 512), half(512, 512),
             half(512, 512), vm(512, 512), half(512, 512), half(512, 512), half(512, 512), half(512, 512),
-            dma(4, 2, 3), dma(4, 2, 3), dma(6, 2, 7), dma(6, 2, 7), dma(10, 2), dma(31), dma(31), dma(3), dma(3),
-            dma(4),
+            dma(4, 2, 3), dma(4, 2, 3), dma(6, 2, 7), dma(6, 2, 7), dma(10, 2), dma(13), dma(13),
+            dma(6),
         ],
         name="step" + str(cap),
         compiler_params=pltpu.CompilerParams(collective_id=ident, has_side_effects=True, vmem_limit_bytes=(44 if cap == CAP else 63) * 2**20),
-    )(assign, assign, gradient, left_stat, right_stat)
+    )(assign, gradient, left_stat, right_stat)
 
 
 def store_kernel(update_in, left_in, right_in, update_out, left_out, right_out):

time: 76.7 us -> 76.7 us (level); the launches traced: 75.7 us -> 76.5 us
  Pallas kernels: 73.9 us -> 74.7 us
    pallas_call x1, Pallas kernels: 70.6 us -> 71.4 us  [step(): pl.pallas_call(functools.partial(step_kernel, cap), out_shape=(jax.ShapeD...]
where the time goes in v5:
time: 76.7 us; the launch traced here: 76.5 us
  Pallas kernels  74.7 us (97%)
  between operations  1.31 us (2%)
    pallas_call x1, Pallas kernels, step(): pl.pallas_call(functools.partial(step_kernel, cap), out_shape=(jax.ShapeD...  71.4 us
    pallas_call x1, Pallas kernels, store(): pl.pallas_call(store_kernel, grid=(3,), out_shape=tuple((jax.ShapeDtypeSt...  3.29 us

profile of v5, /device:TPU:1, one launch (start us, length us, event | category | flops | bytes accessed | tf_op | source)
XLA Modules:
  0.0 76.5 jit_solution(6293210896006759418)
XLA Ops:
  0.6 0.0 copy-start.3
  0.6 71.4 %step8.1 = (f32[1,32,16,512]{3,2,1,0:T(8,128)S(1)}, f32[1,3,512,512]{3,2,1,0:T(8,128)S(1)}, f32[1,3,512,512]{3,2,1,0:T(8,128)S(1)}, f32[8,128]{1,0:T(8,128)S(1)}) custom-call(s32[1,96]{1,0:T(1,128)} %slots_ref.1, f32[1,32,16,512]{3,2,1,0:T(8,128)} %gradient_ref.1, f32[1,3,512,512]{3,2,1,0:T(8,128)} %left_ref.1, f32[1,3,512,512]{3,2,1,0:T(8,128)} %right_ref.1), custom_call_target="tpu_custom_call" | custom-call | tf_op jit(solution)/shard_map/step8/pallas_call | solution.py:437
  72.0 0.5 slice.3
  73.2 0.0 copy-done.3
  73.2 3.3 %store.3 = (f32[1,32,16,512]{3,2,1,0:T(8,128)}, f32[1,3,512,512]{3,2,1,0:T(8,128)}, f32[1,3,512,512]{3,2,1,0:T(8,128)}) custom-call(f32[1,32,16,512]{3,2,1,0:T(8,128)S(1)} %get-tuple-element.29.update_in, f32[1,3,512,512]{3,2,1,0:T(8,128)S(1)} %get-tuple-element.30.left_in, f32[1,3,512,512]{3,2,1,0:T(8,128)S(1)} %get-tuple-element.31.right_in), custom_call_target="tpu_custom_call" | custom-call | tf_op jit(solution)/shard_map/store/pallas_call | solution.py:474
  (1 shorter events, 0.0 us)
Async XLA Ops:
  0.6 72.6 %copy-start.3 = (s32[1,96]{1,0:T(1,128)S(1)}, s32[1,96]{1,0:T(1,128)}, u32[]{:S(2)}) copy-start(s32[1,96]{1,0:T(1,128)} %slots_ref.1) | copy-start | bytes 1156

commit v6 on v5

--- a/solution.py
+++ b/solution.py
@@ -85,9 +85,9 @@
     slots_ref, gradient_ref, left_ref, right_ref,
     update_ref, new_left_ref, new_right_ref, over_ref,
     sent, mid, pad, held, back, rmid, comp, fin,
-    assign_ref, row_ref, grad_ref, sums, sumv, row, table_v, table_ref,
-    sh, sl, a_buf, xh, xl, yh, yl, base, plh, pll, prh, prl,
-    a_s, a_r, b_s, b_r, loc, sum_s, sum_r, io_in,
+    assign_ref, row_ref, grad_ref, sums, sumv, flags, row, table_v, table_ref,
+    sh, sl, a_buf, base, xh, xl, yh, oh, ol,
+    a_s, a_r, b_s, b_r, loc, sum_s, sum_r, flag_s, flag_r, io_in,
 ):
     e = lax.axis_index("expert")
     me = lax.axis_index("shard")
@@ -163,7 +163,7 @@
         return carry
 
     first, more = pl.ds(0, 8), pl.ds(8, cap)
-    near, ring = (1, 3, 2), (1, 7, 2, 6, 3, 5, 4)
+    near, ring = (2, 1, 3), (4, 3, 5, 2, 6, 1, 7)
 
     def along(r, src, dst):
         out, here = [], []
@@ -228,13 +228,8 @@
     pl.semaphore_wait(barrier, 16)
     start(out_first())
 
-    fill_table(row_ref, table_v, row)
-    lists = pltpu.make_async_copy(table_v, table_ref, io_in.at[3])
-    lists.start()
     squares = lax.fori_loop(0, grad_ref.shape[1], square_sum, jnp.zeros((8, 128), F32), unroll=8)
-    sums[0, 0:1, :] = jnp.sum(squares, axis=0, keepdims=True)
-    sums[0, 1:2, :] = table_v[OVER:OVER + 1, :].astype(F32)
-    sums[0, 2:8, :] = jnp.zeros((6, 128), F32)
+    sums[0] = squares
     sum_copies = []
 
     def sum_send(stage, at, peers):
@@ -257,6 +252,17 @@
         sums[stage + 1] = acc
 
     s0 = sum_send(0, 0, [(lax.rem(e + d, 4), me) for d in range(1, 4)])
+    fill_table(row_ref, table_v, row)
+    lists = pltpu.make_async_copy(table_v, table_ref, io_in.at[3])
+    lists.start()
+    flags[0] = table_v[...].astype(F32)
+    flag_copies = []
+    for d in range(1, 4):
+        flag_copies.append(pltpu.make_async_remote_copy(
+            src_ref=flags.at[0], dst_ref=flags.at[d], send_sem=flag_s.at[d - 1], recv_sem=flag_r.at[d - 1],
+            device_id=(lax.rem(e + d, 4), me), device_id_type=MESH))
+    for copy in flag_copies:
+        copy.start()
     lists.wait()
     lax.fori_loop(0, 4 * cap, build_more, 0, unroll=4)
     sum_take(0, 0, s0)
@@ -278,9 +284,13 @@
     build_pad(2)
     start(to_more(2))
     sum_take(2, 6, s2)
-    mean_square = total(sums[3, 0:1, :]) / (4.0 * 32.0 * 512.0 * 512.0)
+    mean_square = total(sums[3]) / (4.0 * 32.0 * 512.0 * 512.0)
     factor = jnp.minimum(1.0, 1.0 / jnp.sqrt(mean_square + 1e-06))
-    over_ref[...] = sums[3]
+    over = flags[0]
+    for d, copy in enumerate(flag_copies):
+        copy.wait_recv()
+        over = over + flags[d + 1]
+    over_ref[0, 0] = jnp.sum(over[OVER:OVER + 1, 0:1]).astype(jnp.int32)
     for copy in loads:
         copy.wait()
 
@@ -296,51 +306,14 @@
 
     tiles = ((0, 0), (0, 1), (1, 1))
 
-    def root(square, oh, ol):
-        norm = jnp.sqrt(square + 1e-06)
-        inverse = 1.0 / norm
-        for i in range(2):
-            for j in range(2):
-                put(xh, xl, i, j, a_buf[part(i), part(j)] * inverse)
-        for i, j in tiles:
-            low = dot(xh[part(i), :], xl[:, part(j)])
-            other = low if i == j else dot(xh[part(j), :], xl[:, part(i)])
-            value = dot(xh[part(i), :], xh[:, part(j)]) + (low + other.T)
-            both(yh, yl, i, j, value)
-            base[part(i), part(j)] = value
-        for i, j in tiles:
-            x3 = (
-                dot(yh[part(i), :], xh[:, part(j)])
-                + (dot(yh[part(i), :], xl[:, part(j)]) + dot(yl[part(i), :], xh[:, part(j)]))
-            )
-            x1 = a_buf[part(i), part(j)] * inverse
-            x2 = base[part(i), part(j)]
-            value = C1 * x1 + C2 * x2 + C3 * x3
-            if i == j:
-                rows = lax.broadcasted_iota(jnp.int32, (HALF, HALF), 0)
-                cols = lax.broadcasted_iota(jnp.int32, (HALF, HALF), 1)
-                value = value + jnp.where(rows == cols, C0, 0.0)
-            base[part(i), part(j)] = value
-            high = x3.astype(BF16)
-            rest = (C4 * x1 + C5 * x2 + C6 * x3)
-            oh[part(i), part(j)] = high
-            ol[part(i), part(j)] = rest.astype(BF16)
-            if i != j:
-                oh[part(j), part(i)] = x3.T.astype(BF16)
-                ol[part(j), part(i)] = rest.T.astype(BF16)
-        for i, j in tiles:
-            base[part(i), part(j)] += dot(oh[part(i), :], ol[:, part(j)])
-        for i, j in tiles:
-            both(oh, ol, i, j, base[part(i), part(j)])
-        return jnp.sqrt(jnp.sqrt(norm))
-
-    def stat(buf, k, live, high, low):
+    def stat(n, buf, k, live, high, low):
         square = jnp.zeros((1, 1), F32)
 
         def take(i, j, product):
             old = buf[k, part(i), part(j)]
             new = 0.95 * old + product
-            a_buf[part(i), part(j)] = new
+            a_buf[n, part(i), part(j)] = new
+            put(xh.at[n], xl.at[n], i, j, new)
             buf[k, part(i), part(j)] = jnp.where(live, new, old)
             return total(new * new)
 
@@ -352,6 +325,38 @@
             if i != j:
                 square = square + take(j, i, product.T)
         return square
+
+    def second(n, inverse):
+        for i, j in tiles:
+            low = dot(xh[n, part(i), :], xl[n, :, part(j)])
+            other = low if i == j else dot(xh[n, part(j), :], xl[n, :, part(i)])
+            value = (dot(xh[n, part(i), :], xh[n, :, part(j)]) + (low + other.T)) * (inverse * inverse)
+            base[n, part(i), part(j)] = value
+            yh[n, part(i), part(j)] = value.astype(BF16)
+            if i != j:
+                yh[n, part(j), part(i)] = value.T.astype(BF16)
+
+    def third(n, inverse):
+        for i, j in tiles:
+            x3 = (dot(yh[n, part(i), :], xh[n, :, part(j)]) + dot(yh[n, part(i), :], xl[n, :, part(j)])) * inverse
+            x1 = a_buf[n, part(i), part(j)] * inverse
+            x2 = base[n, part(i), part(j)]
+            value = C1 * x1 + C2 * x2 + C3 * x3
+            if i == j:
+                rows = lax.broadcasted_iota(jnp.int32, (HALF, HALF), 0)
+                cols = lax.broadcasted_iota(jnp.int32, (HALF, HALF), 1)
+                value = value + jnp.where(rows == cols, C0, 0.0)
+            base[n, part(i), part(j)] = value
+            rest = C4 * x1 + C5 * x2 + C6 * x3
+            oh[n, part(i), part(j)] = x3.astype(BF16)
+            ol[n, part(i), part(j)] = rest.astype(BF16)
+            if i != j:
+                oh[n, part(j), part(i)] = x3.T.astype(BF16)
+                ol[n, part(j), part(i)] = rest.T.astype(BF16)
+
+    def last(n):
+        for i, j in tiles:
+            both(xh.at[n], xl.at[n], i, j, base[n, part(i), part(j)] + dot(oh[n, part(i), :], ol[n, :, part(j)]))
 
     def slot(k):
         live = assign_ref[0, me * 3 + k] >= 0
@@ -362,32 +367,39 @@
                 graft = graft + total(piece * piece)
                 put(sh, sl, i, j, piece)
         nt, tn = ((1,), (1,)), ((0,), (0,))
-        left_scale = root(stat(
-            lbuf, k, live,
-            lambda i, j: dot(sh[part(i), :], sh[part(j), :], nt),
-            lambda i, j: dot(sh[part(i), :], sl[part(j), :], nt)), plh, pll)
-        right_scale = root(stat(
-            rbuf, k, live,
-            lambda i, j: dot(sh[:, part(i)], sh[:, part(j)], tn),
-            lambda i, j: dot(sh[:, part(i)], sl[:, part(j)], tn)), prh, prl)
-
+        squares = (
+            stat(0, lbuf, k, live,
+                 lambda i, j: dot(sh[part(i), :], sh[part(j), :], nt),
+                 lambda i, j: dot(sh[part(i), :], sl[part(j), :], nt)),
+            stat(1, rbuf, k, live,
+                 lambda i, j: dot(sh[:, part(i)], sh[:, part(j)], tn),
+                 lambda i, j: dot(sh[:, part(i)], sl[:, part(j)], tn)))
+        norms = [jnp.sqrt(square + 1e-06) for square in squares]
+        inverses = [1.0 / norm for norm in norms]
+        for n in range(2):
+            second(n, inverses[n])
+        for n in range(2):
+            third(n, inverses[n])
+        for n in range(2):
+            last(n)
+        scale = 1.0 / (jnp.sqrt(jnp.sqrt(norms[0])) * jnp.sqrt(jnp.sqrt(norms[1])))
+
+        th, tl = oh.at[0], ol.at[0]
         for i in range(2):
             for j in range(2):
-                put(xh, xl, i, j, dot(plh[part(i), :], sh[:, part(j)])
-                    + (dot(plh[part(i), :], sl[:, part(j)]) + dot(pll[part(i), :], sh[:, part(j)])))
+                put(th, tl, i, j, dot(xh[0, part(i), :], sh[:, part(j)])
+                    + (dot(xh[0, part(i), :], sl[:, part(j)]) + dot(xl[0, part(i), :], sh[:, part(j)])))
         square = jnp.zeros((1, 1), F32)
-        scale = 1.0 / (left_scale * right_scale)
         for i in range(2):
             for j in range(2):
-                value = dot(xh[part(i), :], prh[:, part(j)]) + (
-                    dot(xh[part(i), :], prl[:, part(j)]) + dot(xl[part(i), :], prh[:, part(j)]))
-                value = value * scale
+                value = dot(th[part(i), :], xh[1, :, part(j)]) + (
+                    dot(th[part(i), :], xl[1, :, part(j)]) + dot(tl[part(i), :], xh[1, :, part(j)]))
                 square = square + total(value * value)
-                a_buf[part(i), part(j)] = value
+                base[0, part(i), part(j)] = value
         count = 512.0 * 512.0
-        ratio = jnp.sqrt(graft / count + 1e-12) / jnp.sqrt(square / count + 1e-12)
+        ratio = scale * jnp.sqrt(graft / count + 1e-12) / jnp.sqrt(square * (scale * scale) / count + 1e-12)
         for i in range(2):
-            back[k, 2 * i:2 * i + 2] = (a_buf[part(i), :] * ratio).reshape(2, 4, 2, 2, 8, 512)
+            back[k, 2 * i:2 * i + 2] = (base[0, part(i), :] * ratio).reshape(2, 4, 2, 2, 8, 512)
 
     def turn(k, carry):
         landed(arrive(k))
@@ -409,7 +421,7 @@
     gone(to_more(2))
     for k in range(3):
         gone(from_slot(k))
-    for copy in sum_copies:
+    for copy in sum_copies + flag_copies:
         copy.wait_send()
     for copies in (in_first(), in_more()):
         landed(copies)
@@ -440,18 +452,18 @@
             jax.ShapeDtypeStruct(gradient.shape, F32),
             jax.ShapeDtypeStruct(left_stat.shape, F32),
             jax.ShapeDtypeStruct(right_stat.shape, F32),
-            jax.ShapeDtypeStruct((8, 128), F32),
+            jax.ShapeDtypeStruct((1, 1), jnp.int32),
         ),
         in_specs=[any_spec] * 4,
-        out_specs=(vmem, vmem, vmem, vmem),
+        out_specs=(vmem, vmem, vmem, pl.BlockSpec(memory_space=pltpu.SMEM)),
         scratch_shapes=[
             vm(2, 4, entries, 8, 512), vm(2, 4, entries, 8, 512), vm(2, 2, 8, 4, 8, 512), vm(*piece),
             vm(*piece), vm(3, 2, 8, 4, 8, 512), vm(2, 4, cap, 8, 512), vm(2, 4, entries, 8, 512),
-            pltpu.SMEM((1, 96), jnp.int32), vm(1, 96, dtype=jnp.int32), vm(1, 32, 16, 512), vm(4, 8, 128), vm(13, 8, 128),
+            pltpu.SMEM((1, 96), jnp.int32), vm(1, 96, dtype=jnp.int32), vm(1, 32, 16, 512), vm(4, 8, 128), vm(13, 8, 128), vm(4, 8, 128),
             vm(8, 128), vm(8, 128, dtype=jnp.int32), pltpu.SMEM((8, 128), jnp.int32),
-            half(512, 512), half(512, 512), vm(512, 512), half(512, 512), half(512, 512), half(512, 512),
-            half(512, 512), vm(512, 512), half(512, 512), half(512, 512), half(512, 512), half(512, 512),
-            dma(4, 2, 3), dma(4, 2, 3), dma(6, 2, 7), dma(6, 2, 7), dma(10, 2), dma(13), dma(13),
+            half(512, 512), half(512, 512), vm(2, 512, 512), vm(2, 512, 512),
+            half(2, 512, 512), half(2, 512, 512), half(2, 512, 512), half(2, 512, 512), half(2, 512, 512),
+            dma(4, 2, 3), dma(4, 2, 3), dma(6, 2, 7), dma(6, 2, 7), dma(10, 2), dma(13), dma(13), dma(3), dma(3),
             dma(6),
         ],
         name="step" + str(cap),
@@ -488,7 +500,7 @@
     def again(_):
         return store(step(FULL, 1, assign, gradient, left_stat, right_stat)[:3])
 
-    return lax.cond(over[1, 0] > 0.0, again, lambda kept: kept, store(outs))
+    return lax.cond(over[0, 0] > 0, again, lambda kept: kept, store(outs))
 
 
 def solution(mesh):

time: 76.7 us -> 73.4 us (0.957)
  Pallas kernels: 74.7 us -> 72 us
    pallas_call x1, Pallas kernels: 71.4 us -> 68.7 us  [step(): pl.pallas_call(functools.partial(step_kernel, cap), out_shape=(jax.ShapeD...]
where the time goes in v6:
time: 73.4 us; the launch traced here: 73.2 us
  Pallas kernels  72 us (98%)
  between operations  1.21 us (2%)
    pallas_call x1, Pallas kernels, step(): pl.pallas_call(functools.partial(step_kernel, cap), out_shape=(jax.ShapeD...  68.7 us
    pallas_call x1, Pallas kernels, store(): pl.pallas_call(store_kernel, grid=(3,), out_shape=tuple((jax.ShapeDtypeSt...  3.29 us

profile of v6, /device:TPU:1, one launch (start us, length us, event | category | flops | bytes accessed | tf_op | source)
XLA Modules:
  0.0 73.2 jit_solution(7536489825466955153)
XLA Ops:
  0.6 0.0 copy-start.3
  0.6 68.7 %step8.1 = (f32[1,32,16,512]{3,2,1,0:T(8,128)S(1)}, f32[1,3,512,512]{3,2,1,0:T(8,128)S(1)}, f32[1,3,512,512]{3,2,1,0:T(8,128)S(1)}, s32[1,1]{1,0:T(1,128)}) custom-call(s32[1,96]{1,0:T(1,128)} %slots_ref.1, f32[1,32,16,512]{3,2,1,0:T(8,128)} %gradient_ref.1, f32[1,3,512,512]{3,2,1,0:T(8,128)} %left_ref.1, f32[1,3,512,512]{3,2,1,0:T(8,128)} %right_ref.1), custom_call_target="tpu_custom_call" | custom-call | tf_op jit(solution)/shard_map/step8/pallas_call | solution.py:449
  69.9 0.0 copy-done.3
  69.9 3.3 %store.3 = (f32[1,32,16,512]{3,2,1,0:T(8,128)}, f32[1,3,512,512]{3,2,1,0:T(8,128)}, f32[1,3,512,512]{3,2,1,0:T(8,128)}) custom-call(f32[1,32,16,512]{3,2,1,0:T(8,128)S(1)} %get-tuple-element.29.update_in, f32[1,3,512,512]{3,2,1,0:T(8,128)S(1)} %get-tuple-element.30.left_in, f32[1,3,512,512]{3,2,1,0:T(8,128)S(1)} %get-tuple-element.31.right_in), custom_call_target="tpu_custom_call" | custom-call | tf_op jit(solution)/shard_map/store/pallas_call | solution.py:486
  (1 shorter events, 0.0 us)
Async XLA Ops:
  0.6 69.3 %copy-start.3 = (s32[1,96]{1,0:T(1,128)S(1)}, s32[1,96]{1,0:T(1,128)}, u32[]{:S(2)}) copy-start(s32[1,96]{1,0:T(1,128)} %slots_ref.1) | copy-start | bytes 1156

commit v7 on v6

--- a/solution.py
+++ b/solution.py
@@ -224,7 +224,7 @@
 
     for copy in fetches:
         copy.wait()
-    lax.fori_loop(0, 32, build_first, 0, unroll=8)
+    lax.fori_loop(0, 32, build_first, 0, unroll=16)
     pl.semaphore_wait(barrier, 16)
     start(out_first())
 
@@ -330,7 +330,7 @@
         for i, j in tiles:
             low = dot(xh[n, part(i), :], xl[n, :, part(j)])
             other = low if i == j else dot(xh[n, part(j), :], xl[n, :, part(i)])
-            value = (dot(xh[n, part(i), :], xh[n, :, part(j)]) + (low + other.T)) * (inverse * inverse)
+            value = (dot(xh[n, part(i), :], xh[n, :, part(j)]) + (low + other.T)) * inverse * inverse
             base[n, part(i), part(j)] = value
             yh[n, part(i), part(j)] = value.astype(BF16)
             if i != j:
@@ -412,7 +412,7 @@
     start(in_first())
     landed(from_slot(1))
     landed(from_slot(2))
-    lax.fori_loop(0, cap, build_comp, 0, unroll=4)
+    lax.fori_loop(0, cap, build_comp, 0, unroll=8)
     start(in_more())
     gone(out_first())
     gone(out_more())
@@ -435,7 +435,7 @@
             update_ref[0, b, h * 8:h * 8 + 8] = fin[h, a, entry]
         return carry
 
-    lax.fori_loop(0, update_ref.shape[1], take, 0, unroll=4)
+    lax.fori_loop(0, update_ref.shape[1], take, 0, unroll=16)
 
 
 def step(cap, ident, assign, gradient, left_stat, right_stat):

time: 73.4 us -> 73.3 us (level)
  no operation moved by 1% of the time
where the time goes in v7:
time: 73.3 us; the launch traced here: 73.2 us
  Pallas kernels  72 us (98%)
  between operations  1.21 us (2%)
    pallas_call x1, Pallas kernels, step(): pl.pallas_call(functools.partial(step_kernel, cap), out_shape=(jax.ShapeD...  68.7 us
    pallas_call x1, Pallas kernels, store(): pl.pallas_call(store_kernel, grid=(3,), out_shape=tuple((jax.ShapeDtypeSt...  3.29 us

profile of v7, /device:TPU:1, one launch (start us, length us, event | category | flops | bytes accessed | tf_op | source)
XLA Modules:
  0.0 73.2 jit_solution(6828706707470066178)
XLA Ops:
  0.6 0.0 copy-start.3
  0.6 68.7 %step8.1 = (f32[1,32,16,512]{3,2,1,0:T(8,128)S(1)}, f32[1,3,512,512]{3,2,1,0:T(8,128)S(1)}, f32[1,3,512,512]{3,2,1,0:T(8,128)S(1)}, s32[1,1]{1,0:T(1,128)}) custom-call(s32[1,96]{1,0:T(1,128)} %slots_ref.1, f32[1,32,16,512]{3,2,1,0:T(8,128)} %gradient_ref.1, f32[1,3,512,512]{3,2,1,0:T(8,128)} %left_ref.1, f32[1,3,512,512]{3,2,1,0:T(8,128)} %right_ref.1), custom_call_target="tpu_custom_call" | custom-call | tf_op jit(solution)/shard_map/step8/pallas_call | solution.py:449
  69.9 0.0 copy-done.3
  69.9 3.3 %store.3 = (f32[1,32,16,512]{3,2,1,0:T(8,128)}, f32[1,3,512,512]{3,2,1,0:T(8,128)}, f32[1,3,512,512]{3,2,1,0:T(8,128)}) custom-call(f32[1,32,16,512]{3,2,1,0:T(8,128)S(1)} %get-tuple-element.29.update_in, f32[1,3,512,512]{3,2,1,0:T(8,128)S(1)} %get-tuple-element.30.left_in, f32[1,3,512,512]{3,2,1,0:T(8,128)S(1)} %get-tuple-element.31.right_in), custom_call_target="tpu_custom_call" | custom-call | tf_op jit(solution)/shard_map/store/pallas_call | solution.py:486
  (1 shorter events, 0.0 us)
Async XLA Ops:
  0.6 69.2 %copy-start.3 = (s32[1,96]{1,0:T(1,128)S(1)}, s32[1,96]{1,0:T(1,128)}, u32[]{:S(2)}) copy-start(s32[1,96]{1,0:T(1,128)} %slots_ref.1) | copy-start | bytes 1156

commit v8 on v7

--- a/solution.py
+++ b/solution.py
@@ -224,9 +224,16 @@
 
     for copy in fetches:
         copy.wait()
-    lax.fori_loop(0, 32, build_first, 0, unroll=16)
-    pl.semaphore_wait(barrier, 16)
-    start(out_first())
+    firsts, kept = out_first()
+    for n, d in enumerate(near + (0,)):
+        t = lax.rem(z + d, 4)
+        lax.fori_loop(t * 8, t * 8 + 8, build_first, 0)
+        if n == 0:
+            pl.semaphore_wait(barrier, 16)
+        if d:
+            firsts[2 * n].start()
+    for copy in firsts[1::2] + kept:
+        copy.start()
 
     squares = lax.fori_loop(0, grad_ref.shape[1], square_sum, jnp.zeros((8, 128), F32), unroll=8)
     sums[0] = squares

time: 73.3 us -> 73.7 us (level)
  no operation moved by 1% of the time
where the time goes in v8:
time: 73.7 us; the launch traced here: 73.6 us
  Pallas kernels  72.4 us (98%)
  between operations  1.21 us (2%)
    pallas_call x1, Pallas kernels, step(): pl.pallas_call(functools.partial(step_kernel, cap), out_shape=(jax.ShapeD...  69.1 us
    pallas_call x1, Pallas kernels, store(): pl.pallas_call(store_kernel, grid=(3,), out_shape=tuple((jax.ShapeDtypeSt...  3.29 us

profile of v8, /device:TPU:1, one launch (start us, length us, event | category | flops | bytes accessed | tf_op | source)
XLA Modules:
  0.0 73.6 jit_solution(10754291831831418740)
XLA Ops:
  0.6 0.0 copy-start.3
  0.6 69.1 %step8.1 = (f32[1,32,16,512]{3,2,1,0:T(8,128)S(1)}, f32[1,3,512,512]{3,2,1,0:T(8,128)S(1)}, f32[1,3,512,512]{3,2,1,0:T(8,128)S(1)}, s32[1,1]{1,0:T(1,128)}) custom-call(s32[1,96]{1,0:T(1,128)} %slots_ref.1, f32[1,32,16,512]{3,2,1,0:T(8,128)} %gradient_ref.1, f32[1,3,512,512]{3,2,1,0:T(8,128)} %left_ref.1, f32[1,3,512,512]{3,2,1,0:T(8,128)} %right_ref.1), custom_call_target="tpu_custom_call" | custom-call | tf_op jit(solution)/shard_map/step8/pallas_call | solution.py:456
  70.3 0.0 copy-done.3
  70.3 3.3 %store.3 = (f32[1,32,16,512]{3,2,1,0:T(8,128)}, f32[1,3,512,512]{3,2,1,0:T(8,128)}, f32[1,3,512,512]{3,2,1,0:T(8,128)}) custom-call(f32[1,32,16,512]{3,2,1,0:T(8,128)S(1)} %get-tuple-element.29.update_in, f32[1,3,512,512]{3,2,1,0:T(8,128)S(1)} %get-tuple-element.30.left_in, f32[1,3,512,512]{3,2,1,0:T(8,128)S(1)} %get-tuple-element.31.right_in), custom_call_target="tpu_custom_call" | custom-call | tf_op jit(solution)/shard_map/store/pallas_call | solution.py:493
  (1 shorter events, 0.0 us)
Async XLA Ops:
  0.6 69.7 %copy-start.3 = (s32[1,96]{1,0:T(1,128)S(1)}, s32[1,96]{1,0:T(1,128)}, u32[]{:S(2)}) copy-start(s32[1,96]{1,0:T(1,128)} %slots_ref.1) | copy-start | bytes 1156
